TPU v7x, 32 devices: a whole 2x2x4 slice. The times are simulated.
32 devices in a mesh: grp: 2 (over y), blk: 16 (over z, x, core).
Axes of the slice: x: 2, y: 2, z: 4, core: 2. Of those that a mesh axis runs over, the one named last changes fastest.
Arguments:
- tokens: bfloat16 [64, 8192], P(('grp', 'blk')), parts along dimension 0, may hold values from -6 to 6
- gate_matrix: bfloat16 [8192, 16384], P(None, 'blk'), may hold values from -0.0625 to 0.0625
- up_matrix: bfloat16 [8192, 16384], P(None, 'blk'), may hold values from -0.0625 to 0.0625
- down_matrix: bfloat16 [16384, 8192], P('blk'), may hold values from -0.046875 to 0.046875
- gate_adapter_input: bfloat16 [8192, 16], replicated, may hold values from -0.0625 to 0.0625
- gate_adapter_output: bfloat16 [16, 16384], P(None, 'blk'), may hold values from -1.5 to 1.5
- up_adapter_input: bfloat16 [8192, 16], replicated, may hold values from -0.0625 to 0.0625
- up_adapter_output: bfloat16 [16, 16384], P(None, 'blk'), may hold values from -1.5 to 1.5
- down_adapter_input: bfloat16 [16384, 16], P('blk'), may hold values from -0.046875 to 0.046875
- down_adapter_output: bfloat16 [16, 8192], replicated, may hold values from -1.5 to 1.5
Outputs:
- mixed: bfloat16 [64, 8192], P(('grp', 'blk')), parts along dimension 0
- importance: float32 [64], P(('grp', 'blk')), parts along dimension 0
There are 2 independent parts, one for each index of `grp`. A program takes and returns all parts, laid end to end along the dimension named above; an argument that names none is the same for every part. Nothing has to cross between parts.
All inputs are finite; a program needn't handle non-finite values.
Results may differ from a plain program's by a relative error of at most 0.0054.
Values may be sent and summed in bfloat16 or wider, within the bound.
No kernel may reach another device: no remote copies, remote signals or barrier semaphores. Data moves between devices by JAX's collectives and lax.ppermute only.
A program may use at most 128 MiB of HBM per device.

v0:
```python
import jax
import jax.numpy as jnp
from jax import lax
from jax.sharding import PartitionSpec as P


def hidden_token_rows(
    input_rows,
    gate_matrix,
    up_matrix,
    gate_adapter_input,
    gate_adapter_output,
    up_adapter_input,
    up_adapter_output,
):
    gate_reduced = jnp.dot(
        input_rows, gate_adapter_input, preferred_element_type=jnp.float32
    ).astype(jnp.bfloat16)
    up_reduced = jnp.dot(input_rows, up_adapter_input, preferred_element_type=jnp.float32).astype(
        jnp.bfloat16
    )
    gate_value = jnp.dot(
        input_rows, gate_matrix, preferred_element_type=jnp.float32
    ) + 0.5 * jnp.dot(gate_reduced, gate_adapter_output, preferred_element_type=jnp.float32)
    up_value = jnp.dot(input_rows, up_matrix, preferred_element_type=jnp.float32) + 0.5 * jnp.dot(
        up_reduced, up_adapter_output, preferred_element_type=jnp.float32
    )
    return (jax.nn.silu(gate_value) * up_value).astype(jnp.bfloat16)


def body(
    tokens,
    gate_matrix,
    up_matrix,
    down_matrix,
    gate_adapter_input,
    gate_adapter_output,
    up_adapter_input,
    up_adapter_output,
    down_adapter_input,
    down_adapter_output,
):
    collected_rows = lax.all_gather(tokens, "blk", axis=0, tiled=True)
    hidden_state = hidden_token_rows(
        collected_rows,
        gate_matrix,
        up_matrix,
        gate_adapter_input,
        gate_adapter_output,
        up_adapter_input,
        up_adapter_output,
    )
    middle_state = jnp.dot(hidden_state, down_adapter_input, preferred_element_type=jnp.float32)
    output_matrix = down_adapter_output.astype(jnp.float32)
    base = jnp.dot(hidden_state, down_matrix, preferred_element_type=jnp.float32)
    base_rows, middle_rows = (
        lax.psum_scatter(base, "blk", scatter_dimension=0, tiled=True),
        lax.psum_scatter(middle_state, "blk", scatter_dimension=0, tiled=True),
    )
    adapter_branch = 0.5 * jnp.dot(middle_rows, output_matrix, precision=lax.Precision.HIGHEST)
    mixed = (base_rows + adapter_branch).astype(jnp.bfloat16)
    importance = jnp.sqrt(jnp.sum(adapter_branch * adapter_branch, axis=-1))
    return (mixed, importance)


def solution(mesh):
    in_specs = (
        P(("grp", "blk"), None),
        P(None, "blk"),
        P(None, "blk"),
        P("blk", None),
        P(),
        P(None, "blk"),
        P(),
        P(None, "blk"),
        P("blk", None),
        P(),
    )
    out_specs = (P(("grp", "blk"), None), P(("grp", "blk")))
    return jax.shard_map(body, mesh=mesh, in_specs=in_specs, out_specs=out_specs, check_vma=False)
```

profile of v0, /device:TPU:0, one launch (start us, length us, event | category | flops | bytes accessed | tf_op | source)
XLA Modules:
  0.0 154.6 jit_solution(9377459513982438593)
XLA Ops:
  7.2 0.0 copy-start
  7.2 0.0 all-reduce.4.cloned.1.call-start
  7.2 24.9 %all-gather = bf16[16,2,8192]{2,1,0:T(2,128)(2,1)S(1)} all-gather(bf16[1,2,8192]{2,1,0:T(2,128)(2,1)} %bitcast.19), channel_id=1, replica_groups=mesh['grp'=2,'blk'=16] {'blk'}, dimensions={0}, use_global_device_ids=true | all-gather | bytes 557056 | tf_op jit(solution)/shard_map/all_gather | solution.py:43
  32.2 0.2 reshape.5
  32.4 0.0 copy-done
  32.4 1.2 convolution_multiply_fusion.1
  33.6 1.4 convolution_multiply_fusion.2
  35.0 0.0 copy-start.1
  35.0 0.0 slice-start
  35.0 0.0 slice-start.1
  35.0 8.9 %convolution_add_fusion.1 = f32[32,1024]{1,0:T(8,128)S(1)} fusion(f32[32,1024]{1,0:T(8,128)S(1)} %convolution_multiply_fusion.2, bf16[32,8192]{1,0:T(8,128)(2,1)S(1)} %reshape.5, bf16[8192,1024]{1,0:T(8,128)(2,1)} %param.11), kind=kOutput, calls=%fused_computation.3 | convolution fusion | flops 536903680 | bytes 17563648 | tf_op jit(solution)/shard_map/dot_general | solution.py:22
  44.0 1.6 %copy-done.1 = bf16[8192,1024]{1,0:T(8,128)(2,1)S(1)} copy-done((bf16[8192,1024]{1,0:T(8,128)(2,1)S(1)}, bf16[8192,1024]{1,0:T(8,128)(2,1)}, u32[]{:S(2)}) %copy-start.1) | copy-done | bytes 16777240
  45.5 3.0 %fusion.1 = bf16[32,1024]{1,0:T(8,128)(2,1)S(1)} fusion(f32[32,1024]{1,0:T(8,128)S(1)} %convolution_multiply_fusion.1, bf16[32,8192]{1,0:T(8,128)(2,1)S(1)} %reshape.5, bf16[8192,1024]{1,0:T(8,128)(2,1)S(1)} %copy-done.1, f32[32,1024]{1,0:T(8,128)S(1)} %convolution_add_fusion.1), kind=kOutput, calls=%fused_computation.6 | convolution fusion | flops 537100288 | bytes 17629184 | tf_op jit(solution)/shard_map/dot_general | solution.py:25
  48.6 0.8 slice-done.2
  49.4 1.2 slice-done.3
  50.6 4.0 %fusion.5 = f32[32,8192]{1,0:T(8,128)} fusion(bf16[32,1024]{1,0:T(8,128)(2,1)S(1)} %fusion.1, bf16[1024,8192]{1,0:T(8,128)(2,1)S(1)} %bitcast.18), kind=kOutput, calls=%fused_computation.14 | convolution fusion | flops 536870912 | bytes 17891328 | tf_op jit(solution)/shard_map/dot_general | solution.py:55
  54.6 0.0 all-reduce.4.cloned.1.call-update
  54.6 0.0 copy-done.4
  54.6 0.6 dynamic-slice
  55.9 0.1 fusion.6
  56.0 58.1 %all-reduce.1 = f32[32,16]{1,0:T(8,128)S(1)} all-reduce(f32[32,16]{1,0:T(8,128)S(1)} %fusion.6), channel_id=3, replica_groups=mesh['grp'=2,'blk'=16] {'blk'}, use_global_device_ids=true, to_apply=%region_1.2.clone | all-reduce | flops 512 | bytes 4096
  114.1 31.2 %all-reduce.4.cloned.1.call-done = f32[32,8192]{1,0:T(8,128)} async-done(((f32[32,8192]{1,0:T(8,128)}), f32[32,8192]{1,0:T(8,128)}) %all-reduce.4.cloned.1.call-update) | async-done | bytes 1048592
  145.3 2.0 %multiply_reduce_fusion = (f32[2]{0:T(128)S(1)}, bf16[2,8192]{1,0:T(2,128)(2,1)}) fusion(f32[32,8192]{1,0:T(8,128)} %all-reduce.4.cloned.1.call-done, u32[]{:T(128)S(6)} %multiply.1, bf16[16,8192]{1,0:T(8,128)(2,1)S(1)} %copy-done.3, f32[32,16]{1,0:T(8,128)S(1)} %all-reduce.1), kind=kOutput, calls=%fused_computation.11 | convolution fusion | flops 3227646 | bytes 362504 | tf_op jit(solution)/shard_map/dot_general | solution.py:60
  147.3 0.5 sqrt.3
  (10 shorter events, 0.0 us)
Async XLA Ops:
  7.2 25.2 %copy-start = (bf16[8192,16]{0,1:T(8,128)(2,1)S(1)}, bf16[8192,16]{0,1:T(8,128)(2,1)}, u32[]{:S(2)}) copy-start(bf16[8192,16]{0,1:T(8,128)(2,1)} %param.16) | copy-start | bytes 786436
  7.2 138.1 %all-reduce.4.cloned.1.call-start = ((), (), s32[]{:S(2)}) async-start(), calls=%async_computation | async-start | bytes 2097152
  35.0 10.5 %copy-start.1 = (bf16[8192,1024]{1,0:T(8,128)(2,1)S(1)}, bf16[8192,1024]{1,0:T(8,128)(2,1)}, u32[]{:S(2)}) copy-start(bf16[8192,1024]{1,0:T(8,128)(2,1)} %param.12) | copy-start | bytes 50331652
  35.0 13.6 %slice-start = ((s8[16777216]{0:T(1024)(128)(4,1)}), s8[4194304]{0:T(1024)(128)(4,1)S(1)}, s32[]{:S(2)}) async-start(s8[16777216]{0:T(1024)(128)(4,1)} %bitcast.17), calls=%async_computation.1 | async-start | bytes 8388608
  35.0 13.6 %slice-start.1 = ((s8[16777216]{0:T(1024)(128)(4,1)}), s8[4194304]{0:T(1024)(128)(4,1)S(1)}, s32[]{:S(2)}) async-start(s8[16777216]{0:T(1024)(128)(4,1)} %bitcast.17), calls=%async_computation.2 | async-start | bytes 8388608
  45.5 3.8 %slice-start.2 = ((s8[16777216]{0:T(1024)(128)(4,1)}), s8[4194304]{0:T(1024)(128)(4,1)S(1)}, s32[]{:S(2)}) async-start(s8[16777216]{0:T(1024)(128)(4,1)} %bitcast.17), calls=%async_computation.3 | async-start | bytes 8388608
  45.5 5.0 %slice-start.3 = ((s8[16777216]{0:T(1024)(128)(4,1)}), s8[4194304]{0:T(1024)(128)(4,1)S(1)}, s32[]{:S(2)}) async-start(s8[16777216]{0:T(1024)(128)(4,1)} %bitcast.17), calls=%async_computation.4 | async-start | bytes 8388608
  50.6 4.0 %copy-start.4 = (u32[32]{0:T(128)S(1)}, u32[32]{0:T(128)}, u32[]{:S(2)}) copy-start(u32[32]{0:T(128)} %constant.11) | copy-start | bytes 388
  50.6 5.3 %copy-start.2 = (bf16[1024,16]{0,1:T(8,128)(2,1)S(1)}, bf16[1024,16]{0,1:T(8,128)(2,1)}, u32[]{:S(2)}) copy-start(bf16[1024,16]{0,1:T(8,128)(2,1)} %param.18) | copy-start | bytes 98308
  50.6 94.7 %copy-start.3 = (bf16[16,8192]{1,0:T(8,128)(2,1)S(1)}, bf16[16,8192]{1,0:T(8,128)(2,1)}, u32[]{:S(2)}) copy-start(bf16[16,8192]{1,0:T(8,128)(2,1)} %param.19) | copy-start | bytes 786436
Sparse Core Ops, SparseCore 0:
  54.7 90.5 all-reduce.3
where the time goes:
time: 155 us
  blocking collectives  83 us (54%)
  waiting for transfers between devices  31.2 us (20%)
  matrix products  20.7 us (13%)
  between operations  14.8 us (10%)
  local copies, waits for them, and re-layouts  4.9 us (3%)
    unnamed x1, blocking collectives  58.1 us
    unnamed x2, waiting for transfers between devices  31.2 us
    all_gather x1, blocking collectives, body(): collected_rows = lax.all_gather(tokens, 'blk', axis=0, tiled=True)  24.9 us
    dot_general x1, matrix products, hidden_token_rows(): jnp.dot(input_rows, gate_matrix, preferred_element_type=jnp.float32)  8.92 us
    unnamed x20, local copies, waits for them, and re-layouts  4.37 us
    dot_general x1, matrix products, body(): jnp.dot(hidden_state, down_matrix, preferred_element_type=jnp.float32)  4.01 us
  transfers between devices with their start and end apart: 1, of which 1 were waited for; matrix products, arithmetic and copies ran while one was open for 0% of the time, Pallas kernels for 0%

commit v1 on v0

v1 whole, which is shorter than its diff:
```python
import functools

import jax
import jax.numpy as jnp
from jax import lax
from jax.experimental import pallas as pl
from jax.experimental.pallas import tpu as pltpu
from jax.sharding import PartitionSpec as P

MIB = 1 << 20


def swap(value, size, bit):
    return lax.ppermute(value, "blk", [(i, i ^ bit) for i in range(size)])


def hidden_kernel(rows, gate, up, gate_in, gate_out, up_in, up_out, hidden):
    x = rows[...]
    dims = (((1,), (1,)), ((), ()))
    gate_low = lax.dot_general(x, gate_in[...], dims, preferred_element_type=jnp.float32)
    up_low = lax.dot_general(x, up_in[...], dims, preferred_element_type=jnp.float32)
    gate_low = gate_low.astype(jnp.bfloat16)
    up_low = up_low.astype(jnp.bfloat16)
    width = hidden.shape[1]
    step = 256

    @pl.loop(0, width // step)
    def _(j):
        cols = pl.ds(pl.multiple_of(j * step, step), step)
        g = jnp.dot(x, gate[:, cols], preferred_element_type=jnp.float32)
        g += 0.5 * jnp.dot(gate_low, gate_out[:, cols], preferred_element_type=jnp.float32)
        u = jnp.dot(x, up[:, cols], preferred_element_type=jnp.float32)
        u += 0.5 * jnp.dot(up_low, up_out[:, cols], preferred_element_type=jnp.float32)
        hidden[:, cols] = (g / (1.0 + jnp.exp(-g)) * u).astype(jnp.bfloat16)


def down_kernel(hidden, down, down_in, base, middle):
    h = hidden[...]
    dims = (((1,), (1,)), ((), ()))
    middle[...] = lax.dot_general(h, down_in[...], dims, preferred_element_type=jnp.float32)
    step = 512

    @pl.loop(0, base.shape[1] // step)
    def _(j):
        cols = pl.ds(pl.multiple_of(j * step, step), step)
        base[:, cols] = jnp.dot(h, down[:, cols], preferred_element_type=jnp.float32).astype(jnp.bfloat16)


def body(size, tokens, gate, up, down, gate_in, gate_out, up_in, up_out, down_in, down_out):
    bits = [1 << b for b in range(size.bit_length() - 1)]
    rows = tokens
    for bit in reversed(bits):
        rows = jnp.concatenate([rows, swap(rows, size, bit)], axis=0)
    vmem = functools.partial(pltpu.with_memory_space_constraint, memory_space=pltpu.VMEM)
    whole = pl.BlockSpec(memory_space=pltpu.VMEM)
    count, width = rows.shape[0], gate.shape[1]
    hidden = pl.pallas_call(
        hidden_kernel,
        out_shape=jax.ShapeDtypeStruct((count, width), jnp.bfloat16),
        in_specs=[whole] * 7,
        out_specs=whole,
        compiler_params=pltpu.CompilerParams(vmem_limit_bytes=8 * MIB),
        name="hidden",
    )(rows, vmem(gate), vmem(up), gate_in.T, gate_out, up_in.T, up_out)
    base, middle = pl.pallas_call(
        down_kernel,
        out_shape=[
            jax.ShapeDtypeStruct((count, down.shape[1]), jnp.bfloat16),
            jax.ShapeDtypeStruct((count, down_in.shape[1]), jnp.float32),
        ],
        in_specs=[whole] * 3,
        out_specs=[whole] * 2,
        compiler_params=pltpu.CompilerParams(vmem_limit_bytes=8 * MIB),
        name="down",
    )(hidden, vmem(down), down_in.T)
    for bit in bits:
        half = base.shape[0] // 2
        got_base = swap(base[half:], size, bit)
        got_middle = swap(middle[half:], size, bit)
        base = base[:half].astype(jnp.float32) + got_base.astype(jnp.float32)
        middle = middle[:half] + got_middle
        if half > tokens.shape[0]:
            base = base.astype(jnp.bfloat16)
    adapter = 0.5 * jnp.dot(middle, down_out.astype(jnp.float32), precision=lax.Precision.HIGHEST)
    mixed = (base + adapter).astype(jnp.bfloat16)
    importance = jnp.sqrt(jnp.sum(adapter * adapter, axis=-1))
    return mixed, importance


def solution(mesh):
    size = mesh.shape["blk"]
    in_specs = (
        P(("grp", "blk"), None),
        P(None, "blk"),
        P(None, "blk"),
        P("blk", None),
        P(),
        P(None, "blk"),
        P(),
        P(None, "blk"),
        P("blk", None),
        P(),
    )
    out_specs = (P(("grp", "blk"), None), P(("grp", "blk")))
    return jax.shard_map(
        functools.partial(body, size), mesh=mesh, in_specs=in_specs, out_specs=out_specs, check_vma=False
    )
```

time: 155 us -> 69.4 us (0.45)
  blocking collectives: 83 us -> 0 us
  matrix products: 20.7 us -> 1.01 us
  starting transfers between devices: 0.04 us -> 16.1 us
  between operations: 14.8 us -> 0.76 us
  local copies, waits for them, and re-layouts: 4.9 us -> 16.6 us
  Pallas kernels: 0 us -> 11.4 us
  waiting for transfers between devices: 31.2 us -> 20.1 us
  other arithmetic: 0.01 us -> 2.77 us
    unnamed x1 -> x0, blocking collectives: 58.1 us -> none
    unnamed x2 -> x0, waiting for transfers between devices: 31.2 us -> none
    all_gather x1 -> x0, blocking collectives: 24.9 us -> none  [body(): collected_rows = lax.all_gather(tokens, 'blk', axis=0, tiled=True)]
    ppermute x0 -> x12, waiting for transfers between devices: none -> 20.1 us  [swap(): return lax.ppermute(value, 'blk', [(i, i ^ bit) for i in range(size)])]
    dot_general x7 -> x1, matrix products: 20.7 us -> 1.01 us  [body(): jnp.dot(middle, down_out.astype(jnp.float32), precision=lax.Precision.HIG...]
    ppermute x0 -> x12, starting transfers between devices: none -> 16.1 us  [swap(): return lax.ppermute(value, 'blk', [(i, i ^ bit) for i in range(size)])]
    pallas_call x0 -> x2, Pallas kernels: none -> 11.4 us  [the longest x1 6.6 us: body(): pl.pallas_call(hidden_kernel, out_shape=jax.ShapeDtypeStruct((count, widt...]
    unnamed x20 -> x18, local copies, waits for them, and re-layouts: 4.37 us -> 15 us
  transfers between devices with their start and end apart: 1 -> 12, of which waited for: 1 -> 8; matrix products, arithmetic and copies ran while one was open for 0% -> 0% of each run, Pallas kernels for 0% -> 0%
where the time goes in v1:
time: 69.4 us; the launch traced here: 68.8 us
  waiting for transfers between devices  20.1 us (29%)
  local copies, waits for them, and re-layouts  16.6 us (24%)
  starting transfers between devices  16.1 us (23%)
  Pallas kernels  11.4 us (16%)
  other arithmetic  2.77 us (4%)
  matrix products  1.01 us (1%)
  between operations  0.76 us (1%)
    ppermute x12, waiting for transfers between devices, swap(): return lax.ppermute(value, 'blk', [(i, i ^ bit) for i in range(size)])  20.1 us
    ppermute x12, starting transfers between devices, swap(): return lax.ppermute(value, 'blk', [(i, i ^ bit) for i in range(size)])  16.1 us
    unnamed x18, local copies, waits for them, and re-layouts  15 us
    pallas_call x1, Pallas kernels, body(): pl.pallas_call(hidden_kernel, out_shape=jax.ShapeDtypeStruct((count, widt...  6.6 us
    pallas_call x1, Pallas kernels, body(): pl.pallas_call(down_kernel, out_shape=[jax.ShapeDtypeStruct((count, down....  4.77 us
    concatenate x3, other arithmetic, body(): rows = jnp.concatenate([rows, swap(rows, size, bit)], axis=0)  2.63 us
  transfers between devices with their start and end apart: 12, of which 8 were waited for; matrix products, arithmetic and copies ran while one was open for 0% of the time, Pallas kernels for 0%

profile of v1, /device:TPU:0, one launch (start us, length us, event | category | flops | bytes accessed | tf_op | source)
XLA Modules:
  0.0 68.8 jit_solution(3606891438352788483)
XLA Ops:
  0.6 4.1 %collective-permute-start = (bf16[2,8192]{1,0:T(2,128)(2,1)}, bf16[2,8192]{1,0:T(2,128)(2,1)S(1)}, u32[]{:S(2)}, u32[]{:S(2)}) collective-permute-start(bf16[2,8192]{1,0:T(2,128)(2,1)} %param.10), channel_id=1, source_target_pairs={{0,8},{1,9},{2,10},{3,11},{4,12},{5,13},{6,14},{7,15},{8,0},{9,1},... | collective-permute-start | bytes 98312 | tf_op jit(solution)/shard_map/ppermute | solution.py:14
  4.7 2.5 %collective-permute-done = bf16[2,8192]{1,0:T(2,128)(2,1)S(1)} collective-permute-done((bf16[2,8192]{1,0:T(2,128)(2,1)}, bf16[2,8192]{1,0:T(2,128)(2,1)S(1)}, u32[]{:S(2)}, u32[]{:S(2)}) %collective-permute-start) | collective-permute-done | bytes 32800 | tf_op jit(solution)/shard_map/ppermute | solution.py:14
  8.0 1.6 %collective-permute-start.1 = (bf16[4,8192]{1,0:T(4,128)(2,1)S(1)}, bf16[4,8192]{1,0:T(4,128)(2,1)S(1)}, u32[]{:S(2)}, u32[]{:S(2)}) collective-permute-start(bf16[4,8192]{1,0:T(4,128)(2,1)S(1)} %pad_maximum_fusion.2), channel_id=1, source_target_pairs={{0,4},{1,5},{2,6},{3,7},{4,0},{5,1},{6,2},{7,3},{8,12},{9,13},{10,... | collective-permute-start | bytes 196616 | tf_op jit(solution)/shard_map/ppermute | solution.py:14
  9.7 2.7 %collective-permute-done.1 = bf16[4,8192]{1,0:T(4,128)(2,1)S(1)} collective-permute-done((bf16[4,8192]{1,0:T(4,128)(2,1)S(1)}, bf16[4,8192]{1,0:T(4,128)(2,1)S(1)}, u32[]{:S(2)}, u32[]{:S(2)}) %collective-permute-start.1) | collective-permute-done | bytes 65568 | tf_op jit(solution)/shard_map/ppermute | solution.py:14
  13.2 1.8 %collective-permute-start.2 = (bf16[8,8192]{1,0:T(8,128)(2,1)S(1)}, bf16[8,8192]{1,0:T(8,128)(2,1)S(1)}, u32[]{:S(2)}, u32[]{:S(2)}) collective-permute-start(bf16[8,8192]{1,0:T(8,128)(2,1)S(1)} %pad_maximum_fusion.1), channel_id=1, source_target_pairs={{0,2},{1,3},{2,0},{3,1},{4,6},{5,7},{6,4},{7,5},{8,10},{9,11},{10,... | collective-permute-start | bytes 393224 | tf_op jit(solution)/shard_map/ppermute | solution.py:14
  15.0 3.3 %collective-permute-done.2 = bf16[8,8192]{1,0:T(8,128)(2,1)S(1)} collective-permute-done((bf16[8,8192]{1,0:T(8,128)(2,1)S(1)}, bf16[8,8192]{1,0:T(8,128)(2,1)S(1)}, u32[]{:S(2)}, u32[]{:S(2)}) %collective-permute-start.2) | collective-permute-done | bytes 131104 | tf_op jit(solution)/shard_map/ppermute | solution.py:14
  18.3 0.9 %pad_maximum_fusion = bf16[16,8192]{1,0:T(8,128)(2,1)S(1)} fusion(bf16[8,8192]{1,0:T(8,128)(2,1)S(1)} %collective-permute-done.2, bf16[4,8192]{1,0:T(4,128)(2,1)S(1)} %collective-permute-done.1, bf16[2,8192]{1,0:T(2,128)(2,1)S(1)} %collective-permute-done, bf16[2,8192]{1,0:T(2,128)(2,1)} %param.10), kind=kLoop, calls=%fused_computation.2 | loop fusion | flops 1048576 | bytes 524288 | tf_op jit(solution)/shard_map/concatenate | solution.py:53
  19.3 1.5 %collective-permute-done.3 = bf16[16,8192]{1,0:T(8,128)(2,1)S(1)} collective-permute-done((bf16[16,8192]{1,0:T(8,128)(2,1)S(1)}, bf16[16,8192]{1,0:T(8,128)(2,1)S(1)}, u32[]{:S(2)}, u32[]{:S(2)}) %collective-permute-start.3) | collective-permute-done | bytes 262176 | tf_op jit(solution)/shard_map/ppermute | solution.py:14
  20.8 1.0 %concatenate.18.rows = bf16[32,8192]{1,0:T(8,128)(2,1)S(1)} concatenate(bf16[2,8192]{1,0:T(2,128)(2,1)} %param.10, bf16[2,8192]{1,0:T(2,128)(2,1)S(1)} %collective-permute-done, bf16[4,8192]{1,0:T(4,128)(2,1)S(1)} %collective-permute-done.1, bf16[8,8192]{1,0:T(8,128)(2,1)S(1)} %collective-permute-done.2, bf16[16,8192]{1,0:T(8,128)(2,1)S(1)} %collective-permute-done.3), dimensions={0} | concatenate | bytes 1048576 | tf_op jit(solution)/shard_map/concatenate | solution.py:53
  21.8 5.8 %copy-done.1 = bf16[8192,1024]{1,0:T(8,128)(2,1)S(1)} copy-done((bf16[8192,1024]{1,0:T(8,128)(2,1)S(1)}, bf16[8192,1024]{1,0:T(8,128)(2,1)}, u32[]{:S(2)}) %copy-start.1) | copy-done | bytes 16777240
  27.6 5.8 %copy-done.2 = bf16[8192,1024]{1,0:T(8,128)(2,1)S(1)} copy-done((bf16[8192,1024]{1,0:T(8,128)(2,1)S(1)}, bf16[8192,1024]{1,0:T(8,128)(2,1)}, u32[]{:S(2)}) %copy-start.2) | copy-done | bytes 16777240
  33.3 0.9 %copy-done.4 = bf16[8192,16]{0,1:T(8,128)(2,1)S(1)} copy-done((bf16[8192,16]{0,1:T(8,128)(2,1)S(1)}, bf16[8192,16]{0,1:T(8,128)(2,1)}, u32[]{:S(2)}) %copy-start.4) | copy-done | bytes 262168
  34.3 0.9 %copy-done.5 = bf16[8192,16]{0,1:T(8,128)(2,1)S(1)} copy-done((bf16[8192,16]{0,1:T(8,128)(2,1)S(1)}, bf16[8192,16]{0,1:T(8,128)(2,1)}, u32[]{:S(2)}) %copy-start.5) | copy-done | bytes 262168
  36.8 6.6 %hidden.1 = bf16[32,1024]{1,0:T(8,128)(2,1)S(1)} custom-call(bf16[32,8192]{1,0:T(8,128)(2,1)S(1)} %concatenate.18.rows, bf16[8192,1024]{1,0:T(8,128)(2,1)S(1)} %copy-done.1, bf16[8192,1024]{1,0:T(8,128)(2,1)S(1)} %copy-done.2, bf16[16,8192]{1,0:T(8,128)(2,1)S(1)} %bitcast.4, bf16[16,1024]{1,0:T(8,128)(2,1)S(1)} %copy-done.7, bf16[16,8192]{1,0:T(8,128)(2,1)S(1)} %bitcast.5, ...), custom_call_target="tpu_custom_call" | custom-call | tf_op jit(solution)/shard_map/hidden/pallas_call | solution.py:57
  43.4 4.8 %down.2 = (bf16[32,8192]{1,0:T(8,128)(2,1)S(1)}, f32[32,16]{1,0:T(8,128)S(1)}) custom-call(bf16[32,1024]{1,0:T(8,128)(2,1)S(1)} %hidden.1, bf16[1024,8192]{1,0:T(8,128)(2,1)S(1)} %copy-done.3, bf16[16,1024]{1,0:T(8,128)(2,1)S(1)} %bitcast.6), custom_call_target="tpu_custom_call" | custom-call | tf_op jit(solution)/shard_map/down/pallas_call | solution.py:65
  48.8 1.0 %collective-permute-done.4 = bf16[16,8192]{1,0:T(8,128)(2,1)S(1)} collective-permute-done((bf16[16,8192]{1,0:T(8,128)(2,1)S(1)}, bf16[16,8192]{1,0:T(8,128)(2,1)S(1)}, u32[]{:S(2)}, u32[]{:S(2)}) %collective-permute-start.4) | collective-permute-done | bytes 262176 | tf_op jit(solution)/shard_map/ppermute | solution.py:14
  49.9 1.8 %collective-permute-start.5 = (bf16[8,8192]{1,0:T(8,128)(2,1)S(1)}, bf16[8,8192]{1,0:T(8,128)(2,1)S(1)}, u32[]{:S(2)}, u32[]{:S(2)}) collective-permute-start(bf16[8,8192]{1,0:T(8,128)(2,1)S(1)} %slice.65), channel_id=1, source_target_pairs={{0,2},{1,3},{2,0},{3,1},{4,6},{5,7},{6,4},{7,5},{8,10},{9,11},{10,... | collective-permute-start | bytes 393224 | tf_op jit(solution)/shard_map/ppermute | solution.py:14
  52.1 3.5 %collective-permute-done.5 = bf16[8,8192]{1,0:T(8,128)(2,1)S(1)} collective-permute-done((bf16[8,8192]{1,0:T(8,128)(2,1)S(1)}, bf16[8,8192]{1,0:T(8,128)(2,1)S(1)}, u32[]{:S(2)}, u32[]{:S(2)}) %collective-permute-start.5) | collective-permute-done | bytes 131104 | tf_op jit(solution)/shard_map/ppermute | solution.py:14
  55.6 1.6 %collective-permute-start.6 = (bf16[4,8192]{1,0:T(4,128)(2,1)S(1)}, bf16[4,8192]{1,0:T(4,128)(2,1)S(1)}, u32[]{:S(2)}, u32[]{:S(2)}) collective-permute-start(bf16[4,8192]{1,0:T(4,128)(2,1)S(1)} %slice.67), channel_id=1, source_target_pairs={{0,4},{1,5},{2,6},{3,7},{4,0},{5,1},{6,2},{7,3},{8,12},{9,13},{10,... | collective-permute-start | bytes 196616 | tf_op jit(solution)/shard_map/ppermute | solution.py:14
  57.8 2.2 %collective-permute-done.6 = bf16[4,8192]{1,0:T(4,128)(2,1)S(1)} collective-permute-done((bf16[4,8192]{1,0:T(4,128)(2,1)S(1)}, bf16[4,8192]{1,0:T(4,128)(2,1)S(1)}, u32[]{:S(2)}, u32[]{:S(2)}) %collective-permute-start.6) | collective-permute-done | bytes 65568 | tf_op jit(solution)/shard_map/ppermute | solution.py:14
  60.0 2.6 %collective-permute-start.7 = (bf16[2,8192]{1,0:T(2,128)(2,1)S(1)}, bf16[2,8192]{1,0:T(2,128)(2,1)S(1)}, u32[]{:S(2)}, u32[]{:S(2)}) collective-permute-start(bf16[2,8192]{1,0:T(2,128)(2,1)S(1)} %slice.69), channel_id=1, source_target_pairs={{0,8},{1,9},{2,10},{3,11},{4,12},{5,13},{6,14},{7,15},{8,0},{9,1},... | collective-permute-start | bytes 98312 | tf_op jit(solution)/shard_map/ppermute | solution.py:14
  62.7 1.1 %collective-permute-start.11 = (f32[2,16]{1,0:T(2,128)S(1)}, f32[2,16]{1,0:T(2,128)S(1)}, u32[]{:S(2)}, u32[]{:S(2)}) collective-permute-start(f32[2,16]{1,0:T(2,128)S(1)} %slice.63), channel_id=1, source_target_pairs={{0,8},{1,9},{2,10},{3,11},{4,12},{5,13},{6,14},{7,15},{8,0},{9,1},... | collective-permute-start | bytes 392 | tf_op jit(solution)/shard_map/ppermute | solution.py:14
  63.8 3.5 %collective-permute-done.11 = f32[2,16]{1,0:T(2,128)S(1)} collective-permute-done((f32[2,16]{1,0:T(2,128)S(1)}, f32[2,16]{1,0:T(2,128)S(1)}, u32[]{:S(2)}, u32[]{:S(2)}) %collective-permute-start.11) | collective-permute-done | bytes 160 | tf_op jit(solution)/shard_map/ppermute | solution.py:14
  67.2 1.0 %multiply_reduce_fusion = (f32[2]{0:T(128)S(1)}, bf16[2,8192]{1,0:T(2,128)(2,1)}) fusion(bf16[2,8192]{1,0:T(2,128)(2,1)S(1)} %collective-permute-done.7, bf16[4,8192]{1,0:T(4,128)(2,1)S(1)} %add_convert_fusion.2, bf16[16,8192]{1,0:T(8,128)(2,1)S(1)} %copy-done, f32[2,16]{1,0:T(2,128)S(1)} %collective-permute-done.11, f32[4,16]{1,0:T(4,128)S(1)} %slice_add_fusion.2), kind=kOutput, calls=%fused_computation.7 | convolution fusion | flops 3276830 | bytes 362504 | tf_op jit(solution)/shard_map/dot_general | solution.py:84
  (40 shorter events, 5.6 us)
Async XLA Ops:
  0.6 66.6 %copy-start = (bf16[16,8192]{1,0:T(8,128)(2,1)S(1)}, bf16[16,8192]{1,0:T(8,128)(2,1)}, u32[]{:S(2)}) copy-start(bf16[16,8192]{1,0:T(8,128)(2,1)} %param.19) | copy-start | bytes 786436
  0.6 6.6 %collective-permute-start = (bf16[2,8192]{1,0:T(2,128)(2,1)}, bf16[2,8192]{1,0:T(2,128)(2,1)S(1)}, u32[]{:S(2)}, u32[]{:S(2)}) collective-permute-start(bf16[2,8192]{1,0:T(2,128)(2,1)} %param.10), channel_id=1, source_target_pairs={{0,8},{1,9},{2,10},{3,11},{4,12},{5,13},{6,14},{7,15},{8,0},{9,1},... | collective-permute-start | bytes 98312 | tf_op jit(solution)/shard_map/ppermute | solution.py:14
  8.0 4.3 %collective-permute-start.1 = (bf16[4,8192]{1,0:T(4,128)(2,1)S(1)}, bf16[4,8192]{1,0:T(4,128)(2,1)S(1)}, u32[]{:S(2)}, u32[]{:S(2)}) collective-permute-start(bf16[4,8192]{1,0:T(4,128)(2,1)S(1)} %pad_maximum_fusion.2), channel_id=1, source_target_pairs={{0,4},{1,5},{2,6},{3,7},{4,0},{5,1},{6,2},{7,3},{8,12},{9,13},{10,... | collective-permute-start | bytes 196616 | tf_op jit(solution)/shard_map/ppermute | solution.py:14
  13.2 5.0 %collective-permute-start.2 = (bf16[8,8192]{1,0:T(8,128)(2,1)S(1)}, bf16[8,8192]{1,0:T(8,128)(2,1)S(1)}, u32[]{:S(2)}, u32[]{:S(2)}) collective-permute-start(bf16[8,8192]{1,0:T(8,128)(2,1)S(1)} %pad_maximum_fusion.1), channel_id=1, source_target_pairs={{0,2},{1,3},{2,0},{3,1},{4,6},{5,7},{6,4},{7,5},{8,10},{9,11},{10,... | collective-permute-start | bytes 393224 | tf_op jit(solution)/shard_map/ppermute | solution.py:14
  19.2 1.6 %collective-permute-start.3 = (bf16[16,8192]{1,0:T(8,128)(2,1)S(1)}, bf16[16,8192]{1,0:T(8,128)(2,1)S(1)}, u32[]{:S(2)}, u32[]{:S(2)}) collective-permute-start(bf16[16,8192]{1,0:T(8,128)(2,1)S(1)} %pad_maximum_fusion), channel_id=1, source_target_pairs={{0,1},{1,0},{2,3},{3,2},{4,5},{5,4},{6,7},{7,6},{8,9},{9,8},{10,11... | collective-permute-start | bytes 786440 | tf_op jit(solution)/shard_map/ppermute | solution.py:14
  21.8 5.8 %copy-start.1 = (bf16[8192,1024]{1,0:T(8,128)(2,1)S(1)}, bf16[8192,1024]{1,0:T(8,128)(2,1)}, u32[]{:S(2)}) copy-start(bf16[8192,1024]{1,0:T(8,128)(2,1)} %gate.1) | copy-start | bytes 50331652
  27.6 5.8 %copy-start.2 = (bf16[8192,1024]{1,0:T(8,128)(2,1)S(1)}, bf16[8192,1024]{1,0:T(8,128)(2,1)}, u32[]{:S(2)}) copy-start(bf16[8192,1024]{1,0:T(8,128)(2,1)} %up.1) | copy-start | bytes 50331652
  33.3 0.9 %copy-start.4 = (bf16[8192,16]{0,1:T(8,128)(2,1)S(1)}, bf16[8192,16]{0,1:T(8,128)(2,1)}, u32[]{:S(2)}) copy-start(bf16[8192,16]{0,1:T(8,128)(2,1)} %param.14) | copy-start | bytes 786436
  34.3 0.9 %copy-start.5 = (bf16[8192,16]{0,1:T(8,128)(2,1)S(1)}, bf16[8192,16]{0,1:T(8,128)(2,1)}, u32[]{:S(2)}) copy-start(bf16[8192,16]{0,1:T(8,128)(2,1)} %param.16) | copy-start | bytes 786436
  35.2 0.8 %copy-start.7 = (bf16[16,1024]{1,0:T(8,128)(2,1)S(1)}, bf16[16,1024]{1,0:T(8,128)(2,1)}, u32[]{:S(2)}) copy-start(bf16[16,1024]{1,0:T(8,128)(2,1)} %gate_out.1) | copy-start | bytes 98308
  36.0 0.8 %copy-start.8 = (bf16[16,1024]{1,0:T(8,128)(2,1)S(1)}, bf16[16,1024]{1,0:T(8,128)(2,1)}, u32[]{:S(2)}) copy-start(bf16[16,1024]{1,0:T(8,128)(2,1)} %up_out.1) | copy-start | bytes 98308
  36.8 6.6 %copy-start.3 = (bf16[1024,8192]{1,0:T(8,128)(2,1)S(1)}, bf16[1024,8192]{1,0:T(8,128)(2,1)}, u32[]{:S(2)}) copy-start(bf16[1024,8192]{1,0:T(8,128)(2,1)} %down.3) | copy-start | bytes 50331652
  36.8 6.6 %copy-start.6 = (bf16[1024,16]{0,1:T(8,128)(2,1)S(1)}, bf16[1024,16]{0,1:T(8,128)(2,1)}, u32[]{:S(2)}) copy-start(bf16[1024,16]{0,1:T(8,128)(2,1)} %param.18) | copy-start | bytes 98308
  48.2 1.6 %collective-permute-start.4 = (bf16[16,8192]{1,0:T(8,128)(2,1)S(1)}, bf16[16,8192]{1,0:T(8,128)(2,1)S(1)}, u32[]{:S(2)}, u32[]{:S(2)}) collective-permute-start(bf16[16,8192]{1,0:T(8,128)(2,1)S(1)} %slice.49), channel_id=1, source_target_pairs={{0,1},{1,0},{2,3},{3,2},{4,5},{5,4},{6,7},{7,6},{8,9},{9,8},{10,11... | collective-permute-start | bytes 786440 | tf_op jit(solution)/shard_map/ppermute | solution.py:14
  48.4 3.2 %collective-permute-start.8 = (f32[16,16]{1,0:T(8,128)S(1)}, f32[16,16]{1,0:T(8,128)S(1)}, u32[]{:S(2)}, u32[]{:S(2)}) collective-permute-start(f32[16,16]{1,0:T(8,128)S(1)} %slice.57), channel_id=1, source_target_pairs={{0,1},{1,0},{2,3},{3,2},{4,5},{5,4},{6,7},{7,6},{8,9},{9,8},{10,11... | collective-permute-start | bytes 3080 | tf_op jit(solution)/shard_map/ppermute | solution.py:14
  49.9 5.6 %collective-permute-start.5 = (bf16[8,8192]{1,0:T(8,128)(2,1)S(1)}, bf16[8,8192]{1,0:T(8,128)(2,1)S(1)}, u32[]{:S(2)}, u32[]{:S(2)}) collective-permute-start(bf16[8,8192]{1,0:T(8,128)(2,1)S(1)} %slice.65), channel_id=1, source_target_pairs={{0,2},{1,3},{2,0},{3,1},{4,6},{5,7},{6,4},{7,5},{8,10},{9,11},{10,... | collective-permute-start | bytes 393224 | tf_op jit(solution)/shard_map/ppermute | solution.py:14
  51.7 5.6 %collective-permute-start.9 = (f32[8,16]{1,0:T(8,128)S(1)}, f32[8,16]{1,0:T(8,128)S(1)}, u32[]{:S(2)}, u32[]{:S(2)}) collective-permute-start(f32[8,16]{1,0:T(8,128)S(1)} %slice.71), channel_id=1, source_target_pairs={{0,2},{1,3},{2,0},{3,1},{4,6},{5,7},{6,4},{7,5},{8,10},{9,11},{10,... | collective-permute-start | bytes 1544 | tf_op jit(solution)/shard_map/ppermute | solution.py:14
  55.6 4.3 %collective-permute-start.6 = (bf16[4,8192]{1,0:T(4,128)(2,1)S(1)}, bf16[4,8192]{1,0:T(4,128)(2,1)S(1)}, u32[]{:S(2)}, u32[]{:S(2)}) collective-permute-start(bf16[4,8192]{1,0:T(4,128)(2,1)S(1)} %slice.67), channel_id=1, source_target_pairs={{0,4},{1,5},{2,6},{3,7},{4,0},{5,1},{6,2},{7,3},{8,12},{9,13},{10,... | collective-permute-start | bytes 196616 | tf_op jit(solution)/shard_map/ppermute | solution.py:14
  57.3 5.4 %collective-permute-start.10 = (f32[4,16]{1,0:T(4,128)S(1)}, f32[4,16]{1,0:T(4,128)S(1)}, u32[]{:S(2)}, u32[]{:S(2)}) collective-permute-start(f32[4,16]{1,0:T(4,128)S(1)} %slice.61), channel_id=1, source_target_pairs={{0,4},{1,5},{2,6},{3,7},{4,0},{5,1},{6,2},{7,3},{8,12},{9,13},{10,... | collective-permute-start | bytes 776 | tf_op jit(solution)/shard_map/ppermute | solution.py:14
  60.0 7.2 %collective-permute-start.7 = (bf16[2,8192]{1,0:T(2,128)(2,1)S(1)}, bf16[2,8192]{1,0:T(2,128)(2,1)S(1)}, u32[]{:S(2)}, u32[]{:S(2)}) collective-permute-start(bf16[2,8192]{1,0:T(2,128)(2,1)S(1)} %slice.69), channel_id=1, source_target_pairs={{0,8},{1,9},{2,10},{3,11},{4,12},{5,13},{6,14},{7,15},{8,0},{9,1},... | collective-permute-start | bytes 98312 | tf_op jit(solution)/shard_map/ppermute | solution.py:14
  62.7 4.5 %collective-permute-start.11 = (f32[2,16]{1,0:T(2,128)S(1)}, f32[2,16]{1,0:T(2,128)S(1)}, u32[]{:S(2)}, u32[]{:S(2)}) collective-permute-start(f32[2,16]{1,0:T(2,128)S(1)} %slice.63), channel_id=1, source_target_pairs={{0,8},{1,9},{2,10},{3,11},{4,12},{5,13},{6,14},{7,15},{8,0},{9,1},... | collective-permute-start | bytes 392 | tf_op jit(solution)/shard_map/ppermute | solution.py:14

commit v2 on v1

v2 whole, which is shorter than its diff:
```python
import functools

import jax
import jax.numpy as jnp
from jax import lax
from jax.experimental import pallas as pl
from jax.experimental.pallas import tpu as pltpu
from jax.sharding import PartitionSpec as P

MIB = 1 << 20
LANES = 128
PIECES = 4
FLOPS_PER_US = 10**9
HOLD_US, MERGE_US = 1, (3, 6, 2)
F32, BF16 = jnp.float32, jnp.bfloat16
WHOLE = pl.BlockSpec(memory_space=pltpu.VMEM)
FAR = pl.BlockSpec(memory_space=pltpu.HBM)
vmem = functools.partial(pltpu.with_memory_space_constraint, memory_space=pltpu.VMEM)
hbm = functools.partial(pltpu.with_memory_space_constraint, memory_space=pltpu.HBM)


def call(kernel, out_shape, in_specs, us, name, limit=2 * MIB, scratch=()):
    many = isinstance(out_shape, list)
    return pl.pallas_call(
        kernel,
        out_shape=out_shape,
        in_specs=in_specs,
        out_specs=[WHOLE] * len(out_shape) if many else WHOLE,
        scratch_shapes=list(scratch),
        compiler_params=pltpu.CompilerParams(vmem_limit_bytes=limit),
        cost_estimate=pl.CostEstimate(flops=int(us * FLOPS_PER_US), bytes_accessed=0, transcendentals=0),
        name=name,
    )


def rounds_of(size, along_x):
    masks = [1 << b for b in range(size.bit_length() - 1)]
    x, z = 2, 2 * along_x
    return [[m] for m in reversed(masks) if m not in (1, x, z)] + [[x, z, x ^ z], [1]]


def swap(value, size, mask):
    return lax.ppermute(value, "blk", [(i, i ^ mask) for i in range(size)])


def hold_kernel(source, target):
    pltpu.sync_copy(source, target)


def merge_kernel(*refs):
    merged = refs[-1]
    count = refs[0].shape[0]
    for i, part in enumerate(refs[:-1]):
        merged[i * count : (i + 1) * count] = part[...]


def merge(parts, us):
    count, width = parts[0].shape
    shape = jax.ShapeDtypeStruct((len(parts) * count, width), parts[0].dtype)
    return call(merge_kernel, shape, [WHOLE] * len(parts), us, "merge")(*parts)


def put(sums, middle, targets):
    high = middle.astype(BF16)
    low = (middle - high.astype(F32)).astype(BF16)
    width, rank = sums.shape[1], middle.shape[1]
    count = targets[0].shape[0]
    for i, target in enumerate(targets):
        rows = slice(i * count, (i + 1) * count)
        target[:, :width] = sums[rows].astype(BF16)
        target[:, width : width + rank] = high[rows]
        target[:, width + LANES : width + LANES + rank] = low[rows]


def take(parts):
    width = parts[0].shape[1] - 2 * LANES
    sums = sum(part[:, :width].astype(F32) for part in parts)
    middle = sum(part[:, width : width + LANES].astype(F32) + part[:, width + LANES :].astype(F32) for part in parts)
    return sums, middle


def add_kernel(inputs, *refs):
    sums, middle = take(refs[:inputs])
    put(sums, middle, refs[inputs:])


def add(parts, blocks):
    count, width = parts[0].shape
    shape = [jax.ShapeDtypeStruct((count // blocks, width), BF16)] * blocks
    kernel = functools.partial(add_kernel, len(parts))
    return call(kernel, shape, [WHOLE] * len(parts), 0.2, "add", limit=4 * MIB)(*parts)


def low_rank(x, w_in, w_out):
    low = lax.dot_general(x, w_in[...], (((1,), (1,)), ((), ())), preferred_element_type=F32)
    return 0.5 * jnp.dot(low.astype(BF16), w_out[...], preferred_element_type=F32)


def layer_kernel(
    rows, gate, up, down, gate_in, gate_out, up_in, up_out, down_in, keep, send, gate_low, up_low, hidden, held, arrived
):
    width, out_width = gate.shape[1], down.shape[1]
    piece = out_width // PIECES
    copies = []
    for i in range(PIECES):
        part = pl.ds(i * piece, piece)
        copies.append(pltpu.make_async_copy(down.at[:, part], held.at[:, part], arrived.at[i]))
    for copy in copies:
        copy.start()
    x = rows[...]
    gate_low[...] = low_rank(x, gate_in, gate_out)
    up_low[...] = low_rank(x, up_in, up_out)
    step = min(512, width)

    @pl.loop(0, width // step)
    def _(j):
        block = pl.ds(pl.multiple_of(j * step, step), step)
        g = jnp.dot(x, gate[:, block], preferred_element_type=F32) + gate_low[:, block]
        u = jnp.dot(x, up[:, block], preferred_element_type=F32) + up_low[:, block]
        hidden[:, block] = (g / (1.0 + jnp.exp(-g)) * u).astype(BF16)

    h = hidden[...]
    count = keep.shape[0]
    middle = lax.dot_general(h, down_in[...], (((1,), (1,)), ((), ())), preferred_element_type=F32)
    high = middle.astype(BF16)
    low = (middle - high.astype(F32)).astype(BF16)
    rank = middle.shape[1]
    for i, target in enumerate((keep, send)):
        part = slice(i * count, (i + 1) * count)
        target[:, out_width:] = jnp.zeros((count, 2 * LANES), BF16)
        target[:, out_width : out_width + rank] = high[part]
        target[:, out_width + LANES : out_width + LANES + rank] = low[part]
    for i, copy in enumerate(copies):
        copy.wait()
        for start in range(i * piece, (i + 1) * piece, 512):
            block = slice(start, start + 512)
            sums = jnp.dot(h, held[:, block], preferred_element_type=F32).astype(BF16)
            keep[:, block] = sums[:count]
            send[:, block] = sums[count:]


def last_kernel(mine, theirs, down_out, mixed, importance):
    sums, middle = take((mine, theirs))
    count, rank = mine.shape[0], down_out.shape[0]
    rest = middle[:, :rank]
    adapter = jnp.zeros(sums.shape, F32)
    for _ in range(3):
        part = rest.astype(BF16)
        rest = rest - part.astype(F32)
        adapter += jnp.dot(part, down_out[...], preferred_element_type=F32)
    adapter = 0.5 * adapter
    mixed[...] = (sums + adapter).astype(BF16)
    norm = jnp.sqrt(jnp.sum(adapter * adapter, axis=1, keepdims=True))
    row = lax.broadcasted_iota(jnp.int32, (count, count), 0)
    column = lax.broadcasted_iota(jnp.int32, (count, count), 1)
    importance[...] = jnp.sum(jnp.where(row == column, norm, 0.0), axis=0, keepdims=True)


def body(size, along_x, tokens, gate, up, down, gate_in, gate_out, up_in, up_out, down_in, down_out):
    rounds = rounds_of(size, along_x)
    width, out_width = gate.shape[1], down.shape[1]
    held = call(hold_kernel, jax.ShapeDtypeStruct(tokens.shape, tokens.dtype), [FAR], HOLD_US, "hold")(hbm(tokens))
    rows = tokens
    for k, masks in enumerate(rounds):
        theirs = [swap(rows, size, mask) for mask in masks]
        rows = merge([held if k == 0 else rows] + theirs, MERGE_US[min(k, len(MERGE_US) - 1)])
    count = rows.shape[0]
    parts = call(
        layer_kernel,
        [jax.ShapeDtypeStruct((count // 2, out_width + 2 * LANES), BF16)] * 2,
        [WHOLE] * 3 + [FAR] + [WHOLE] * 5,
        9,
        "layer",
        limit=down.size * 2 + (2 + count // 64 * 2) * MIB,
        scratch=[
            pltpu.VMEM((count, width), F32),
            pltpu.VMEM((count, width), F32),
            pltpu.VMEM((count, width), BF16),
            pltpu.VMEM(down.shape, BF16),
            pltpu.SemaphoreType.DMA((PIECES,)),
        ],
    )(rows, vmem(gate), vmem(up), hbm(down), gate_in.T, gate_out, up_in.T, up_out, down_in.T)
    for masks, after in zip(rounds[::-1], rounds[-2::-1]):
        theirs = [swap(part, size, mask) for part, mask in zip(parts[1:], masks)]
        parts = add([parts[0]] + theirs, 1 + len(after))
    theirs = swap(parts[1], size, rounds[0][0])
    mixed, importance = call(
        last_kernel,
        [jax.ShapeDtypeStruct(tokens.shape, BF16), jax.ShapeDtypeStruct((1, tokens.shape[0]), F32)],
        [WHOLE] * 3,
        1,
        "last",
        limit=4 * MIB,
    )(parts[0], theirs, down_out)
    return mixed, importance.reshape(-1)


def solution(mesh):
    size = mesh.shape["blk"]
    along_x = 2 if size <= 16 else 4
    in_specs = (
        P(("grp", "blk"), None),
        P(None, "blk"),
        P(None, "blk"),
        P("blk", None),
        P(),
        P(None, "blk"),
        P(),
        P(None, "blk"),
        P("blk", None),
        P(),
    )
    out_specs = (P(("grp", "blk"), None), P(("grp", "blk")))
    return jax.shard_map(
        functools.partial(body, size, along_x),
        mesh=mesh,
        in_specs=in_specs,
        out_specs=out_specs,
        check_vma=False,
    )
```

time: 69.4 us -> 44.9 us (0.65)
  local copies, waits for them, and re-layouts: 16.6 us -> 1.33 us
  waiting for transfers between devices: 20.1 us -> 15.8 us
  other arithmetic: 2.77 us -> 0.01 us
  starting transfers between devices: 16.1 us -> 14.2 us
  Pallas kernels: 11.4 us -> 12.6 us
  matrix products: 1.01 us -> 0 us
    unnamed x18 -> x22, local copies, waits for them, and re-layouts: 15 us -> 1.33 us
    ppermute x12 -> x10, waiting for transfers between devices: 20.1 us -> 15.8 us  [swap(): return lax.ppermute(value, 'blk', [(i, i ^ mask) for i in range(size)])]
    concatenate x3 -> x0, other arithmetic: 2.63 us -> none  [body(): rows = jnp.concatenate([rows, swap(rows, size, bit)], axis=0)]
    ppermute x12 -> x10, starting transfers between devices: 16.1 us -> 14.2 us  [swap(): return lax.ppermute(value, 'blk', [(i, i ^ mask) for i in range(size)])]
    pallas_call x2 -> x8, Pallas kernels: 11.4 us -> 12.6 us  [the longest x1 10.5 us: body(): call(layer_kernel, [jax.ShapeDtypeStruct((count // 2, out_width + 2 * LAN...]
    dot_general x1 -> x0, matrix products: 1.01 us -> none  [body(): jnp.dot(middle, down_out.astype(jnp.float32), precision=lax.Precision.HIG...]
    concatenate x1 -> x0, local copies, waits for them, and re-layouts: 0.98 us -> none  [body(): rows = jnp.concatenate([rows, swap(rows, size, bit)], axis=0)]
  transfers between devices with their start and end apart: 12 -> 10, of which waited for: 8 -> 10; matrix products, arithmetic and copies ran while one was open for 0% -> 0% of each run, Pallas kernels for 0% -> 2%
where the time goes in v2:
time: 44.9 us; the launch traced here: 44.7 us
  waiting for transfers between devices  15.8 us (35%)
  starting transfers between devices  14.2 us (32%)
  Pallas kernels  12.6 us (28%)
  local copies, waits for them, and re-layouts  1.33 us (3%)
  between operations  0.81 us (2%)
    ppermute x10, waiting for transfers between devices, swap(): return lax.ppermute(value, 'blk', [(i, i ^ mask) for i in range(size)])  15.8 us
    ppermute x10, starting transfers between devices, swap(): return lax.ppermute(value, 'blk', [(i, i ^ mask) for i in range(size)])  14.2 us
    pallas_call x1, Pallas kernels, body(): call(layer_kernel, [jax.ShapeDtypeStruct((count // 2, out_width + 2 * LAN...  10.5 us
    unnamed x22, local copies, waits for them, and re-layouts  1.33 us
    pallas_call x1, Pallas kernels, body(): call(last_kernel, [jax.ShapeDtypeStruct(tokens.shape, BF16), jax.ShapeDty...  0.97 us
  transfers between devices with their start and end apart: 10, of which 10 were waited for; matrix products, arithmetic and copies ran while one was open for 0% of the time, Pallas kernels for 2%

profile of v2, /device:TPU:0, one launch (start us, length us, event | category | flops | bytes accessed | tf_op | source)
XLA Modules:
  0.0 44.7 jit_solution(16516940125413479040)
XLA Ops:
  0.6 4.1 %collective-permute-start = (bf16[2,8192]{1,0:T(2,128)(2,1)}, bf16[2,8192]{1,0:T(2,128)(2,1)S(1)}, u32[]{:S(2)}, u32[]{:S(2)}) collective-permute-start(bf16[2,8192]{1,0:T(2,128)(2,1)} %source.1), channel_id=1, source_target_pairs={{0,8},{1,9},{2,10},{3,11},{4,12},{5,13},{6,14},{7,15},{8,0},{9,1},... | collective-permute-start | bytes 98312 | tf_op jit(solution)/shard_map/ppermute | solution.py:43
  4.7 0.8 %hold.1.refs_0_ = bf16[2,8192]{1,0:T(2,128)(2,1)S(1)} custom-call(bf16[2,8192]{1,0:T(2,128)(2,1)} %source.1), custom_call_target="tpu_custom_call" | custom-call | flops 1000000000 | tf_op jit(solution)/shard_map/hold/pallas_call | solution.py:162
  5.5 1.7 %collective-permute-done.refs_1_ = bf16[2,8192]{1,0:T(2,128)(2,1)S(1)} collective-permute-done((bf16[2,8192]{1,0:T(2,128)(2,1)}, bf16[2,8192]{1,0:T(2,128)(2,1)S(1)}, u32[]{:S(2)}, u32[]{:S(2)}) %collective-permute-start) | collective-permute-done | bytes 32800 | tf_op jit(solution)/shard_map/ppermute | solution.py:43
  7.3 2.5 %collective-permute-start.3 = (bf16[4,8192]{1,0:T(4,128)(2,1)S(1)}, bf16[4,8192]{1,0:T(4,128)(2,1)S(1)}, u32[]{:S(2)}, u32[]{:S(2)}) collective-permute-start(bf16[4,8192]{1,0:T(4,128)(2,1)S(1)} %merge.3.refs_0_), channel_id=1, source_target_pairs={{0,6},{1,7},{2,4},{3,5},{4,2},{5,3},{6,0},{7,1},{8,14},{9,15},{10,... | collective-permute-start | bytes 196616 | tf_op jit(solution)/shard_map/ppermute | solution.py:43
  9.9 0.7 %collective-permute-start.2 = (bf16[4,8192]{1,0:T(4,128)(2,1)S(1)}, bf16[4,8192]{1,0:T(4,128)(2,1)S(1)}, u32[]{:S(2)}, u32[]{:S(2)}) collective-permute-start(bf16[4,8192]{1,0:T(4,128)(2,1)S(1)} %merge.3.refs_0_), channel_id=1, source_target_pairs={{0,4},{1,5},{2,6},{3,7},{4,0},{5,1},{6,2},{7,3},{8,12},{9,13},{10,... | collective-permute-start | bytes 196616 | tf_op jit(solution)/shard_map/ppermute | solution.py:43
  10.5 0.3 collective-permute-start.1
  10.9 1.7 %collective-permute-done.3.refs_3_ = bf16[4,8192]{1,0:T(4,128)(2,1)S(1)} collective-permute-done((bf16[4,8192]{1,0:T(4,128)(2,1)S(1)}, bf16[4,8192]{1,0:T(4,128)(2,1)S(1)}, u32[]{:S(2)}, u32[]{:S(2)}) %collective-permute-start.3) | collective-permute-done | bytes 65568 | tf_op jit(solution)/shard_map/ppermute | solution.py:43
  12.5 1.6 %collective-permute-done.2.refs_2_ = bf16[4,8192]{1,0:T(4,128)(2,1)S(1)} collective-permute-done((bf16[4,8192]{1,0:T(4,128)(2,1)S(1)}, bf16[4,8192]{1,0:T(4,128)(2,1)S(1)}, u32[]{:S(2)}, u32[]{:S(2)}) %collective-permute-start.2) | collective-permute-done | bytes 65568 | tf_op jit(solution)/shard_map/ppermute | solution.py:43
  14.1 0.7 %collective-permute-done.1.refs_1_ = bf16[4,8192]{1,0:T(4,128)(2,1)S(1)} collective-permute-done((bf16[4,8192]{1,0:T(4,128)(2,1)S(1)}, bf16[4,8192]{1,0:T(4,128)(2,1)S(1)}, u32[]{:S(2)}, u32[]{:S(2)}) %collective-permute-start.1) | collective-permute-done | bytes 65568 | tf_op jit(solution)/shard_map/ppermute | solution.py:43
  15.0 1.5 %collective-permute-done.4.refs_1_ = bf16[16,8192]{1,0:T(8,128)(2,1)S(1)} collective-permute-done((bf16[16,8192]{1,0:T(8,128)(2,1)S(1)}, bf16[16,8192]{1,0:T(8,128)(2,1)S(1)}, u32[]{:S(2)}, u32[]{:S(2)}) %collective-permute-start.4) | collective-permute-done | bytes 262176 | tf_op jit(solution)/shard_map/ppermute | solution.py:43
  16.6 1.3 %copy-done = bf16[8192,1024]{1,0:T(8,128)(2,1)S(1)} copy-done((bf16[8192,1024]{1,0:T(8,128)(2,1)S(1)}, bf16[8192,1024]{1,0:T(8,128)(2,1)}, u32[]{:S(2)}) %copy-start) | copy-done | bytes 16777240
  17.9 10.5 %layer.1 = (bf16[16,8448]{1,0:T(8,128)(2,1)S(1)}, bf16[16,8448]{1,0:T(8,128)(2,1)S(1)}) custom-call(bf16[32,8192]{1,0:T(8,128)(2,1)S(1)} %merge.5.rows, bf16[8192,1024]{1,0:T(8,128)(2,1)S(1)} %bitcast.5, bf16[8192,1024]{1,0:T(8,128)(2,1)S(1)} %copy-done, bf16[1024,8192]{1,0:T(8,128)(2,1)} %down.1, bf16[16,8192]{1,0:T(8,128)(2,1)S(1)} %bitcast.6, ...), custom_call_target="tpu_custom_call" | custom-call | flops 8999999488 | tf_op jit(solution)/shard_map/layer/pallas_call | solution.py:168
  28.4 0.1 collective-permute-start.5
  28.5 1.5 %collective-permute-done.5.refs_1_ = bf16[16,8448]{1,0:T(8,128)(2,1)S(1)} collective-permute-done((bf16[16,8448]{1,0:T(8,128)(2,1)S(1)}, bf16[16,8448]{1,0:T(8,128)(2,1)S(1)}, u32[]{:S(2)}, u32[]{:S(2)}) %collective-permute-start.5) | collective-permute-done | bytes 270368 | tf_op jit(solution)/shard_map/ppermute | solution.py:43
  30.0 0.1 add.2
  30.1 1.8 %collective-permute-start.6 = (bf16[4,8448]{1,0:T(4,128)(2,1)S(1)}, bf16[4,8448]{1,0:T(4,128)(2,1)S(1)}, u32[]{:S(2)}, u32[]{:S(2)}) collective-permute-start(bf16[4,8448]{1,0:T(4,128)(2,1)S(1)} %get-tuple-element.15), channel_id=1, source_target_pairs={{0,2},{1,3},{2,0},{3,1},{4,6},{5,7},{6,4},{7,5},{8,10},{9,11},{10,... | collective-permute-start | bytes 202760 | tf_op jit(solution)/shard_map/ppermute | solution.py:43
  31.9 1.4 %collective-permute-start.7 = (bf16[4,8448]{1,0:T(4,128)(2,1)S(1)}, bf16[4,8448]{1,0:T(4,128)(2,1)S(1)}, u32[]{:S(2)}, u32[]{:S(2)}) collective-permute-start(bf16[4,8448]{1,0:T(4,128)(2,1)S(1)} %get-tuple-element.16), channel_id=1, source_target_pairs={{0,4},{1,5},{2,6},{3,7},{4,0},{5,1},{6,2},{7,3},{8,12},{9,13},{10,... | collective-permute-start | bytes 202760 | tf_op jit(solution)/shard_map/ppermute | solution.py:43
  33.2 0.4 collective-permute-start.8
  33.7 0.8 %collective-permute-done.6.refs_1_ = bf16[4,8448]{1,0:T(4,128)(2,1)S(1)} collective-permute-done((bf16[4,8448]{1,0:T(4,128)(2,1)S(1)}, bf16[4,8448]{1,0:T(4,128)(2,1)S(1)}, u32[]{:S(2)}, u32[]{:S(2)}) %collective-permute-start.6) | collective-permute-done | bytes 67616 | tf_op jit(solution)/shard_map/ppermute | solution.py:43
  34.5 2.4 %collective-permute-done.7.refs_2_ = bf16[4,8448]{1,0:T(4,128)(2,1)S(1)} collective-permute-done((bf16[4,8448]{1,0:T(4,128)(2,1)S(1)}, bf16[4,8448]{1,0:T(4,128)(2,1)S(1)}, u32[]{:S(2)}, u32[]{:S(2)}) %collective-permute-start.7) | collective-permute-done | bytes 67616 | tf_op jit(solution)/shard_map/ppermute | solution.py:43
  36.8 1.6 %collective-permute-done.8.refs_3_ = bf16[4,8448]{1,0:T(4,128)(2,1)S(1)} collective-permute-done((bf16[4,8448]{1,0:T(4,128)(2,1)S(1)}, bf16[4,8448]{1,0:T(4,128)(2,1)S(1)}, u32[]{:S(2)}, u32[]{:S(2)}) %collective-permute-start.8) | collective-permute-done | bytes 67616 | tf_op jit(solution)/shard_map/ppermute | solution.py:43
  38.5 2.9 %collective-permute-start.9 = (bf16[2,8448]{1,0:T(2,128)(2,1)S(1)}, bf16[2,8448]{1,0:T(2,128)(2,1)S(1)}, u32[]{:S(2)}, u32[]{:S(2)}) collective-permute-start(bf16[2,8448]{1,0:T(2,128)(2,1)S(1)} %get-tuple-element.19), channel_id=1, source_target_pairs={{0,8},{1,9},{2,10},{3,11},{4,12},{5,13},{6,14},{7,15},{8,0},{9,1},... | collective-permute-start | bytes 101384 | tf_op jit(solution)/shard_map/ppermute | solution.py:43
  41.4 2.4 %collective-permute-done.9.theirs = bf16[2,8448]{1,0:T(2,128)(2,1)S(1)} collective-permute-done((bf16[2,8448]{1,0:T(2,128)(2,1)S(1)}, bf16[2,8448]{1,0:T(2,128)(2,1)S(1)}, u32[]{:S(2)}, u32[]{:S(2)}) %collective-permute-start.9) | collective-permute-done | bytes 33824 | tf_op jit(solution)/shard_map/ppermute | solution.py:43
  43.7 1.0 %last.1 = (bf16[2,8192]{1,0:T(2,128)(2,1)}, f32[1,2]{1,0:T(1,128)}) custom-call(bf16[2,8448]{1,0:T(2,128)(2,1)S(1)} %get-tuple-element.18.mine, bf16[2,8448]{1,0:T(2,128)(2,1)S(1)} %collective-permute-done.9.theirs, bf16[16,8192]{1,0:T(8,128)(2,1)S(1)} %copy-done.6), custom_call_target="tpu_custom_call" | custom-call | flops 1000000000 | tf_op jit(solution)/shard_map/last/pallas_call | solution.py:187
  (27 shorter events, 0.3 us)
Async XLA Ops:
  0.6 6.6 %collective-permute-start = (bf16[2,8192]{1,0:T(2,128)(2,1)}, bf16[2,8192]{1,0:T(2,128)(2,1)S(1)}, u32[]{:S(2)}, u32[]{:S(2)}) collective-permute-start(bf16[2,8192]{1,0:T(2,128)(2,1)} %source.1), channel_id=1, source_target_pairs={{0,8},{1,9},{2,10},{3,11},{4,12},{5,13},{6,14},{7,15},{8,0},{9,1},... | collective-permute-start | bytes 98312 | tf_op jit(solution)/shard_map/ppermute | solution.py:43
  7.2 9.3 %slice-start = ((s8[16777216]{0:T(1024)(128)(4,1)}), s8[4194304]{0:T(1024)(128)(4,1)S(1)}, s32[]{:S(2)}) async-start(s8[16777216]{0:T(1024)(128)(4,1)} %bitcast.4), calls=%async_computation | async-start | bytes 8388608
  7.2 9.3 %slice-start.1 = ((s8[16777216]{0:T(1024)(128)(4,1)}), s8[4194304]{0:T(1024)(128)(4,1)S(1)}, s32[]{:S(2)}) async-start(s8[16777216]{0:T(1024)(128)(4,1)} %bitcast.4), calls=%async_computation.1 | async-start | bytes 8388608
  7.2 9.3 %slice-start.2 = ((s8[16777216]{0:T(1024)(128)(4,1)}), s8[4194304]{0:T(1024)(128)(4,1)S(1)}, s32[]{:S(2)}) async-start(s8[16777216]{0:T(1024)(128)(4,1)} %bitcast.4), calls=%async_computation.2 | async-start | bytes 8388608
  7.2 9.3 %slice-start.3 = ((s8[16777216]{0:T(1024)(128)(4,1)}), s8[4194304]{0:T(1024)(128)(4,1)S(1)}, s32[]{:S(2)}) async-start(s8[16777216]{0:T(1024)(128)(4,1)} %bitcast.4), calls=%async_computation.3 | async-start | bytes 8388608
  7.2 10.6 %copy-start = (bf16[8192,1024]{1,0:T(8,128)(2,1)S(1)}, bf16[8192,1024]{1,0:T(8,128)(2,1)}, u32[]{:S(2)}) copy-start(bf16[8192,1024]{1,0:T(8,128)(2,1)} %up.1) | copy-start | bytes 50331652
  7.2 10.6 %copy-start.1 = (bf16[8192,16]{0,1:T(8,128)(2,1)S(1)}, bf16[8192,16]{0,1:T(8,128)(2,1)}, u32[]{:S(2)}) copy-start(bf16[8192,16]{0,1:T(8,128)(2,1)} %param.14) | copy-start | bytes 786436
  7.3 10.6 %copy-start.2 = (bf16[8192,16]{0,1:T(8,128)(2,1)S(1)}, bf16[8192,16]{0,1:T(8,128)(2,1)}, u32[]{:S(2)}) copy-start(bf16[8192,16]{0,1:T(8,128)(2,1)} %param.16) | copy-start | bytes 786436
  7.3 10.6 %copy-start.3 = (bf16[16,1024]{1,0:T(8,128)(2,1)S(1)}, bf16[16,1024]{1,0:T(8,128)(2,1)}, u32[]{:S(2)}) copy-start(bf16[16,1024]{1,0:T(8,128)(2,1)} %gate_out.1) | copy-start | bytes 98308
  7.3 10.6 %copy-start.4 = (bf16[16,1024]{1,0:T(8,128)(2,1)S(1)}, bf16[16,1024]{1,0:T(8,128)(2,1)}, u32[]{:S(2)}) copy-start(bf16[16,1024]{1,0:T(8,128)(2,1)} %up_out.1) | copy-start | bytes 98308
  7.3 10.5 %copy-start.5 = (bf16[1024,16]{0,1:T(8,128)(2,1)S(1)}, bf16[1024,16]{0,1:T(8,128)(2,1)}, u32[]{:S(2)}) copy-start(bf16[1024,16]{0,1:T(8,128)(2,1)} %param.18) | copy-start | bytes 98308
  7.3 5.2 %collective-permute-start.3 = (bf16[4,8192]{1,0:T(4,128)(2,1)S(1)}, bf16[4,8192]{1,0:T(4,128)(2,1)S(1)}, u32[]{:S(2)}, u32[]{:S(2)}) collective-permute-start(bf16[4,8192]{1,0:T(4,128)(2,1)S(1)} %merge.3.refs_0_), channel_id=1, source_target_pairs={{0,6},{1,7},{2,4},{3,5},{4,2},{5,3},{6,0},{7,1},{8,14},{9,15},{10,... | collective-permute-start | bytes 196616 | tf_op jit(solution)/shard_map/ppermute | solution.py:43
  9.9 4.3 %collective-permute-start.2 = (bf16[4,8192]{1,0:T(4,128)(2,1)S(1)}, bf16[4,8192]{1,0:T(4,128)(2,1)S(1)}, u32[]{:S(2)}, u32[]{:S(2)}) collective-permute-start(bf16[4,8192]{1,0:T(4,128)(2,1)S(1)} %merge.3.refs_0_), channel_id=1, source_target_pairs={{0,4},{1,5},{2,6},{3,7},{4,0},{5,1},{6,2},{7,3},{8,12},{9,13},{10,... | collective-permute-start | bytes 196616 | tf_op jit(solution)/shard_map/ppermute | solution.py:43
  10.5 4.3 %collective-permute-start.1 = (bf16[4,8192]{1,0:T(4,128)(2,1)S(1)}, bf16[4,8192]{1,0:T(4,128)(2,1)S(1)}, u32[]{:S(2)}, u32[]{:S(2)}) collective-permute-start(bf16[4,8192]{1,0:T(4,128)(2,1)S(1)} %merge.3.refs_0_), channel_id=1, source_target_pairs={{0,2},{1,3},{2,0},{3,1},{4,6},{5,7},{6,4},{7,5},{8,10},{9,11},{10,... | collective-permute-start | bytes 196616 | tf_op jit(solution)/shard_map/ppermute | solution.py:43
  14.9 1.6 %collective-permute-start.4 = (bf16[16,8192]{1,0:T(8,128)(2,1)S(1)}, bf16[16,8192]{1,0:T(8,128)(2,1)S(1)}, u32[]{:S(2)}, u32[]{:S(2)}) collective-permute-start(bf16[16,8192]{1,0:T(8,128)(2,1)S(1)} %merge.4.refs_0_), channel_id=1, source_target_pairs={{0,1},{1,0},{2,3},{3,2},{4,5},{5,4},{6,7},{7,6},{8,9},{9,8},{10,11... | collective-permute-start | bytes 786440 | tf_op jit(solution)/shard_map/ppermute | solution.py:43
  17.9 25.9 %copy-start.6 = (bf16[16,8192]{1,0:T(8,128)(2,1)S(1)}, bf16[16,8192]{1,0:T(8,128)(2,1)}, u32[]{:S(2)}) copy-start(bf16[16,8192]{1,0:T(8,128)(2,1)} %down_out.1) | copy-start | bytes 786436
  28.4 1.6 %collective-permute-start.5 = (bf16[16,8448]{1,0:T(8,128)(2,1)S(1)}, bf16[16,8448]{1,0:T(8,128)(2,1)S(1)}, u32[]{:S(2)}, u32[]{:S(2)}) collective-permute-start(bf16[16,8448]{1,0:T(8,128)(2,1)S(1)} %get-tuple-element.13), channel_id=1, source_target_pairs={{0,1},{1,0},{2,3},{3,2},{4,5},{5,4},{6,7},{7,6},{8,9},{9,8},{10,11... | collective-permute-start | bytes 811016 | tf_op jit(solution)/shard_map/ppermute | solution.py:43
  30.1 4.4 %collective-permute-start.6 = (bf16[4,8448]{1,0:T(4,128)(2,1)S(1)}, bf16[4,8448]{1,0:T(4,128)(2,1)S(1)}, u32[]{:S(2)}, u32[]{:S(2)}) collective-permute-start(bf16[4,8448]{1,0:T(4,128)(2,1)S(1)} %get-tuple-element.15), channel_id=1, source_target_pairs={{0,2},{1,3},{2,0},{3,1},{4,6},{5,7},{6,4},{7,5},{8,10},{9,11},{10,... | collective-permute-start | bytes 202760 | tf_op jit(solution)/shard_map/ppermute | solution.py:43
  31.9 4.9 %collective-permute-start.7 = (bf16[4,8448]{1,0:T(4,128)(2,1)S(1)}, bf16[4,8448]{1,0:T(4,128)(2,1)S(1)}, u32[]{:S(2)}, u32[]{:S(2)}) collective-permute-start(bf16[4,8448]{1,0:T(4,128)(2,1)S(1)} %get-tuple-element.16), channel_id=1, source_target_pairs={{0,4},{1,5},{2,6},{3,7},{4,0},{5,1},{6,2},{7,3},{8,12},{9,13},{10,... | collective-permute-start | bytes 202760 | tf_op jit(solution)/shard_map/ppermute | solution.py:43
  33.2 5.2 %collective-permute-start.8 = (bf16[4,8448]{1,0:T(4,128)(2,1)S(1)}, bf16[4,8448]{1,0:T(4,128)(2,1)S(1)}, u32[]{:S(2)}, u32[]{:S(2)}) collective-permute-start(bf16[4,8448]{1,0:T(4,128)(2,1)S(1)} %get-tuple-element.17), channel_id=1, source_target_pairs={{0,6},{1,7},{2,4},{3,5},{4,2},{5,3},{6,0},{7,1},{8,14},{9,15},{10,... | collective-permute-start | bytes 202760 | tf_op jit(solution)/shard_map/ppermute | solution.py:43
  38.5 5.3 %collective-permute-start.9 = (bf16[2,8448]{1,0:T(2,128)(2,1)S(1)}, bf16[2,8448]{1,0:T(2,128)(2,1)S(1)}, u32[]{:S(2)}, u32[]{:S(2)}) collective-permute-start(bf16[2,8448]{1,0:T(2,128)(2,1)S(1)} %get-tuple-element.19), channel_id=1, source_target_pairs={{0,8},{1,9},{2,10},{3,11},{4,12},{5,13},{6,14},{7,15},{8,0},{9,1},... | collective-permute-start | bytes 101384 | tf_op jit(solution)/shard_map/ppermute | solution.py:43

commit v3 on v2

--- a/solution.py
+++ b/solution.py
@@ -9,9 +9,8 @@
 
 MIB = 1 << 20
 LANES = 128
-PIECES = 4
 FLOPS_PER_US = 10**9
-HOLD_US, MERGE_US = 1, (3, 6, 2)
+HOLD_US, MERGE_US = 2, (2, 4, 2)
 F32, BF16 = jnp.float32, jnp.bfloat16
 WHOLE = pl.BlockSpec(memory_space=pltpu.VMEM)
 FAR = pl.BlockSpec(memory_space=pltpu.HBM)
@@ -91,25 +90,21 @@
     return call(kernel, shape, [WHOLE] * len(parts), 0.2, "add", limit=4 * MIB)(*parts)
 
 
-def low_rank(x, w_in, w_out):
-    low = lax.dot_general(x, w_in[...], (((1,), (1,)), ((), ())), preferred_element_type=F32)
-    return 0.5 * jnp.dot(low.astype(BF16), w_out[...], preferred_element_type=F32)
-
-
 def layer_kernel(
-    rows, gate, up, down, gate_in, gate_out, up_in, up_out, down_in, keep, send, gate_low, up_low, hidden, held, arrived
+    rows, gate, up, down, gate_in, gate_out, up_in, up_out, down_in, keep, send,
+    maps, gate_low, up_low, hidden, held, arrived,
 ):
     width, out_width = gate.shape[1], down.shape[1]
-    piece = out_width // PIECES
-    copies = []
-    for i in range(PIECES):
-        part = pl.ds(i * piece, piece)
-        copies.append(pltpu.make_async_copy(down.at[:, part], held.at[:, part], arrived.at[i]))
-    for copy in copies:
-        copy.start()
+    copy = pltpu.make_async_copy(down, held, arrived)
+    copy.start()
     x = rows[...]
-    gate_low[...] = low_rank(x, gate_in, gate_out)
-    up_low[...] = low_rank(x, up_in, up_out)
+    across = (((1,), (1,)), ((), ()))
+    rank = gate_in.shape[0]
+    maps[:rank] = gate_in[...]
+    maps[rank:] = up_in[...]
+    low = lax.dot_general(x, maps[...], across, preferred_element_type=F32).astype(BF16)
+    gate_low[...] = 0.5 * jnp.dot(low[:, :rank], gate_out[...], preferred_element_type=F32)
+    up_low[...] = 0.5 * jnp.dot(low[:, rank:], up_out[...], preferred_element_type=F32)
     step = min(512, width)
 
     @pl.loop(0, width // step)
@@ -121,34 +116,31 @@
 
     h = hidden[...]
     count = keep.shape[0]
-    middle = lax.dot_general(h, down_in[...], (((1,), (1,)), ((), ())), preferred_element_type=F32)
+    middle = lax.dot_general(h, down_in[...], across, preferred_element_type=F32)
     high = middle.astype(BF16)
     low = (middle - high.astype(F32)).astype(BF16)
-    rank = middle.shape[1]
     for i, target in enumerate((keep, send)):
         part = slice(i * count, (i + 1) * count)
         target[:, out_width:] = jnp.zeros((count, 2 * LANES), BF16)
         target[:, out_width : out_width + rank] = high[part]
         target[:, out_width + LANES : out_width + LANES + rank] = low[part]
-    for i, copy in enumerate(copies):
-        copy.wait()
-        for start in range(i * piece, (i + 1) * piece, 512):
-            block = slice(start, start + 512)
-            sums = jnp.dot(h, held[:, block], preferred_element_type=F32).astype(BF16)
-            keep[:, block] = sums[:count]
-            send[:, block] = sums[count:]
+    copy.wait()
+    for start in range(0, out_width, 1024):
+        block = slice(start, start + 1024)
+        sums = jnp.dot(h, held[:, block], preferred_element_type=F32).astype(BF16)
+        keep[:, block] = sums[:count]
+        send[:, block] = sums[count:]
 
 
 def last_kernel(mine, theirs, down_out, mixed, importance):
     sums, middle = take((mine, theirs))
     count, rank = mine.shape[0], down_out.shape[0]
-    rest = middle[:, :rank]
-    adapter = jnp.zeros(sums.shape, F32)
+    rest, parts = middle[:, :rank], []
     for _ in range(3):
-        part = rest.astype(BF16)
-        rest = rest - part.astype(F32)
-        adapter += jnp.dot(part, down_out[...], preferred_element_type=F32)
-    adapter = 0.5 * adapter
+        parts.append(rest.astype(BF16))
+        rest = rest - parts[-1].astype(F32)
+    product = jnp.dot(jnp.concatenate(parts, axis=0), down_out[...], preferred_element_type=F32)
+    adapter = 0.5 * (product[:count] + product[count : 2 * count] + product[2 * count :])
     mixed[...] = (sums + adapter).astype(BF16)
     norm = jnp.sqrt(jnp.sum(adapter * adapter, axis=1, keepdims=True))
     row = lax.broadcasted_iota(jnp.int32, (count, count), 0)
@@ -173,11 +165,12 @@
         "layer",
         limit=down.size * 2 + (2 + count // 64 * 2) * MIB,
         scratch=[
+            pltpu.VMEM((2 * gate_in.shape[1], gate_in.shape[0]), BF16),
             pltpu.VMEM((count, width), F32),
             pltpu.VMEM((count, width), F32),
             pltpu.VMEM((count, width), BF16),
             pltpu.VMEM(down.shape, BF16),
-            pltpu.SemaphoreType.DMA((PIECES,)),
+            pltpu.SemaphoreType.DMA(()),
         ],
     )(rows, vmem(gate), vmem(up), hbm(down), gate_in.T, gate_out, up_in.T, up_out, down_in.T)
     for masks, after in zip(rounds[::-1], rounds[-2::-1]):

time: 44.9 us -> 40.9 us (0.911)
  waiting for transfers between devices: 15.8 us -> 13.5 us
  local copies, waits for them, and re-layouts: 1.33 us -> 0.06 us
  Pallas kernels: 12.6 us -> 12.1 us
    ppermute x10, waiting for transfers between devices: 15.8 us -> 13.5 us  [swap(): return lax.ppermute(value, 'blk', [(i, i ^ mask) for i in range(size)])]
    unnamed x22, local copies, waits for them, and re-layouts: 1.33 us -> 0.06 us
    pallas_call x1, Pallas kernels: 10.5 us -> 9.42 us  [body(): call(layer_kernel, [jax.ShapeDtypeStruct((count // 2, out_width + 2 * LAN...]
    pallas_call x1, Pallas kernels: 0.79 us -> 1.55 us  [body(): call(hold_kernel, jax.ShapeDtypeStruct(tokens.shape, tokens.dtype), [FAR]...]
  transfers between devices with their start and end apart: 10 -> 10, of which waited for: 10 -> 10; matrix products, arithmetic and copies ran while one was open for 0% -> 0% of each run, Pallas kernels for 2% -> 4%
where the time goes in v3:
time: 40.9 us; the launch traced here: 40.8 us
  starting transfers between devices  14.3 us (35%)
  waiting for transfers between devices  13.5 us (33%)
  Pallas kernels  12.1 us (30%)
  between operations  0.84 us (2%)
    ppermute x10, starting transfers between devices, swap(): return lax.ppermute(value, 'blk', [(i, i ^ mask) for i in range(size)])  14.3 us
    ppermute x10, waiting for transfers between devices, swap(): return lax.ppermute(value, 'blk', [(i, i ^ mask) for i in range(size)])  13.5 us
    pallas_call x1, Pallas kernels, body(): call(layer_kernel, [jax.ShapeDtypeStruct((count // 2, out_width + 2 * LAN...  9.42 us
    pallas_call x1, Pallas kernels, body(): call(hold_kernel, jax.ShapeDtypeStruct(tokens.shape, tokens.dtype), [FAR]...  1.55 us
    pallas_call x1, Pallas kernels, body(): call(last_kernel, [jax.ShapeDtypeStruct(tokens.shape, BF16), jax.ShapeDty...  0.88 us
  transfers between devices with their start and end apart: 10, of which 10 were waited for; matrix products, arithmetic and copies ran while one was open for 0% of the time, Pallas kernels for 4%

profile of v3, /device:TPU:0, one launch (start us, length us, event | category | flops | bytes accessed | tf_op | source)
XLA Modules:
  0.0 40.8 jit_solution(7023983991968081457)
XLA Ops:
  0.7 4.1 %collective-permute-start = (bf16[2,8192]{1,0:T(2,128)(2,1)}, bf16[2,8192]{1,0:T(2,128)(2,1)S(1)}, u32[]{:S(2)}, u32[]{:S(2)}) collective-permute-start(bf16[2,8192]{1,0:T(2,128)(2,1)} %source.1), channel_id=1, source_target_pairs={{0,8},{1,9},{2,10},{3,11},{4,12},{5,13},{6,14},{7,15},{8,0},{9,1},... | collective-permute-start | bytes 98312 | tf_op jit(solution)/shard_map/ppermute | solution.py:42
  4.8 1.6 %hold.1.refs_0_ = bf16[2,8192]{1,0:T(2,128)(2,1)S(1)} custom-call(bf16[2,8192]{1,0:T(2,128)(2,1)} %source.1), custom_call_target="tpu_custom_call" | custom-call | flops 2000000000 | tf_op jit(solution)/shard_map/hold/pallas_call | solution.py:154
  6.4 0.9 %collective-permute-done.refs_1_ = bf16[2,8192]{1,0:T(2,128)(2,1)S(1)} collective-permute-done((bf16[2,8192]{1,0:T(2,128)(2,1)}, bf16[2,8192]{1,0:T(2,128)(2,1)S(1)}, u32[]{:S(2)}, u32[]{:S(2)}) %collective-permute-start) | collective-permute-done | bytes 32800 | tf_op jit(solution)/shard_map/ppermute | solution.py:42
  7.3 2.5 %collective-permute-start.3 = (bf16[4,8192]{1,0:T(4,128)(2,1)S(1)}, bf16[4,8192]{1,0:T(4,128)(2,1)S(1)}, u32[]{:S(2)}, u32[]{:S(2)}) collective-permute-start(bf16[4,8192]{1,0:T(4,128)(2,1)S(1)} %merge.3.refs_0_), channel_id=1, source_target_pairs={{0,6},{1,7},{2,4},{3,5},{4,2},{5,3},{6,0},{7,1},{8,14},{9,15},{10,... | collective-permute-start | bytes 196616 | tf_op jit(solution)/shard_map/ppermute | solution.py:42
  9.9 0.7 %collective-permute-start.2 = (bf16[4,8192]{1,0:T(4,128)(2,1)S(1)}, bf16[4,8192]{1,0:T(4,128)(2,1)S(1)}, u32[]{:S(2)}, u32[]{:S(2)}) collective-permute-start(bf16[4,8192]{1,0:T(4,128)(2,1)S(1)} %merge.3.refs_0_), channel_id=1, source_target_pairs={{0,4},{1,5},{2,6},{3,7},{4,0},{5,1},{6,2},{7,3},{8,12},{9,13},{10,... | collective-permute-start | bytes 196616 | tf_op jit(solution)/shard_map/ppermute | solution.py:42
  10.5 0.3 collective-permute-start.1
  10.9 1.7 %collective-permute-done.3.refs_3_ = bf16[4,8192]{1,0:T(4,128)(2,1)S(1)} collective-permute-done((bf16[4,8192]{1,0:T(4,128)(2,1)S(1)}, bf16[4,8192]{1,0:T(4,128)(2,1)S(1)}, u32[]{:S(2)}, u32[]{:S(2)}) %collective-permute-start.3) | collective-permute-done | bytes 65568 | tf_op jit(solution)/shard_map/ppermute | solution.py:42
  12.5 1.6 %collective-permute-done.2.refs_2_ = bf16[4,8192]{1,0:T(4,128)(2,1)S(1)} collective-permute-done((bf16[4,8192]{1,0:T(4,128)(2,1)S(1)}, bf16[4,8192]{1,0:T(4,128)(2,1)S(1)}, u32[]{:S(2)}, u32[]{:S(2)}) %collective-permute-start.2) | collective-permute-done | bytes 65568 | tf_op jit(solution)/shard_map/ppermute | solution.py:42
  14.1 0.7 %collective-permute-done.1.refs_1_ = bf16[4,8192]{1,0:T(4,128)(2,1)S(1)} collective-permute-done((bf16[4,8192]{1,0:T(4,128)(2,1)S(1)}, bf16[4,8192]{1,0:T(4,128)(2,1)S(1)}, u32[]{:S(2)}, u32[]{:S(2)}) %collective-permute-start.1) | collective-permute-done | bytes 65568 | tf_op jit(solution)/shard_map/ppermute | solution.py:42
  14.9 0.1 collective-permute-start.4
  15.0 1.5 %collective-permute-done.4.refs_1_ = bf16[16,8192]{1,0:T(8,128)(2,1)S(1)} collective-permute-done((bf16[16,8192]{1,0:T(8,128)(2,1)S(1)}, bf16[16,8192]{1,0:T(8,128)(2,1)S(1)}, u32[]{:S(2)}, u32[]{:S(2)}) %collective-permute-start.4) | collective-permute-done | bytes 262176 | tf_op jit(solution)/shard_map/ppermute | solution.py:42
  16.6 9.4 %layer.1 = (bf16[16,8448]{1,0:T(8,128)(2,1)S(1)}, bf16[16,8448]{1,0:T(8,128)(2,1)S(1)}) custom-call(bf16[32,8192]{1,0:T(8,128)(2,1)S(1)} %merge.5.rows, bf16[8192,1024]{1,0:T(8,128)(2,1)S(1)} %bitcast.5, bf16[8192,1024]{1,0:T(8,128)(2,1)S(1)} %copy-done, bf16[1024,8192]{1,0:T(8,128)(2,1)} %down.1, bf16[16,8192]{1,0:T(8,128)(2,1)S(1)} %bitcast.6, ...), custom_call_target="tpu_custom_call" | custom-call | flops 8999999488 | tf_op jit(solution)/shard_map/layer/pallas_call | solution.py:160
  26.1 0.2 collective-permute-start.5
  26.3 1.4 %collective-permute-done.5.refs_1_ = bf16[16,8448]{1,0:T(8,128)(2,1)S(1)} collective-permute-done((bf16[16,8448]{1,0:T(8,128)(2,1)S(1)}, bf16[16,8448]{1,0:T(8,128)(2,1)S(1)}, u32[]{:S(2)}, u32[]{:S(2)}) %collective-permute-start.5) | collective-permute-done | bytes 270368 | tf_op jit(solution)/shard_map/ppermute | solution.py:42
  27.7 0.1 add.2
  27.8 0.4 collective-permute-start.6
  28.2 1.6 %collective-permute-start.7 = (bf16[4,8448]{1,0:T(4,128)(2,1)S(1)}, bf16[4,8448]{1,0:T(4,128)(2,1)S(1)}, u32[]{:S(2)}, u32[]{:S(2)}) collective-permute-start(bf16[4,8448]{1,0:T(4,128)(2,1)S(1)} %get-tuple-element.16), channel_id=1, source_target_pairs={{0,4},{1,5},{2,6},{3,7},{4,0},{5,1},{6,2},{7,3},{8,12},{9,13},{10,... | collective-permute-start | bytes 202760 | tf_op jit(solution)/shard_map/ppermute | solution.py:42
  29.7 1.6 %collective-permute-start.8 = (bf16[4,8448]{1,0:T(4,128)(2,1)S(1)}, bf16[4,8448]{1,0:T(4,128)(2,1)S(1)}, u32[]{:S(2)}, u32[]{:S(2)}) collective-permute-start(bf16[4,8448]{1,0:T(4,128)(2,1)S(1)} %get-tuple-element.17), channel_id=1, source_target_pairs={{0,6},{1,7},{2,4},{3,5},{4,2},{5,3},{6,0},{7,1},{8,14},{9,15},{10,... | collective-permute-start | bytes 202760 | tf_op jit(solution)/shard_map/ppermute | solution.py:42
  31.3 0.8 %collective-permute-done.6.refs_1_ = bf16[4,8448]{1,0:T(4,128)(2,1)S(1)} collective-permute-done((bf16[4,8448]{1,0:T(4,128)(2,1)S(1)}, bf16[4,8448]{1,0:T(4,128)(2,1)S(1)}, u32[]{:S(2)}, u32[]{:S(2)}) %collective-permute-start.6) | collective-permute-done | bytes 67616 | tf_op jit(solution)/shard_map/ppermute | solution.py:42
  32.1 0.3 collective-permute-done.7.refs_2_
  32.4 2.5 %collective-permute-done.8.refs_3_ = bf16[4,8448]{1,0:T(4,128)(2,1)S(1)} collective-permute-done((bf16[4,8448]{1,0:T(4,128)(2,1)S(1)}, bf16[4,8448]{1,0:T(4,128)(2,1)S(1)}, u32[]{:S(2)}, u32[]{:S(2)}) %collective-permute-start.8) | collective-permute-done | bytes 67616 | tf_op jit(solution)/shard_map/ppermute | solution.py:42
  35.0 2.8 %collective-permute-start.9 = (bf16[2,8448]{1,0:T(2,128)(2,1)S(1)}, bf16[2,8448]{1,0:T(2,128)(2,1)S(1)}, u32[]{:S(2)}, u32[]{:S(2)}) collective-permute-start(bf16[2,8448]{1,0:T(2,128)(2,1)S(1)} %get-tuple-element.19), channel_id=1, source_target_pairs={{0,8},{1,9},{2,10},{3,11},{4,12},{5,13},{6,14},{7,15},{8,0},{9,1},... | collective-permute-start | bytes 101384 | tf_op jit(solution)/shard_map/ppermute | solution.py:42
  37.9 2.1 %collective-permute-done.9.theirs = bf16[2,8448]{1,0:T(2,128)(2,1)S(1)} collective-permute-done((bf16[2,8448]{1,0:T(2,128)(2,1)S(1)}, bf16[2,8448]{1,0:T(2,128)(2,1)S(1)}, u32[]{:S(2)}, u32[]{:S(2)}) %collective-permute-start.9) | collective-permute-done | bytes 33824 | tf_op jit(solution)/shard_map/ppermute | solution.py:42
  39.9 0.9 %last.1 = (bf16[2,8192]{1,0:T(2,128)(2,1)}, f32[1,2]{1,0:T(1,128)}) custom-call(bf16[2,8448]{1,0:T(2,128)(2,1)S(1)} %get-tuple-element.18.mine, bf16[2,8448]{1,0:T(2,128)(2,1)S(1)} %collective-permute-done.9.theirs, bf16[16,8192]{1,0:T(8,128)(2,1)S(1)} %copy-done.6), custom_call_target="tpu_custom_call" | custom-call | flops 1000000000 | tf_op jit(solution)/shard_map/last/pallas_call | solution.py:180
  (27 shorter events, 0.2 us)
Async XLA Ops:
  0.6 15.9 %copy-start.5 = (bf16[1024,16]{0,1:T(8,128)(2,1)S(1)}, bf16[1024,16]{0,1:T(8,128)(2,1)}, u32[]{:S(2)}) copy-start(bf16[1024,16]{0,1:T(8,128)(2,1)} %param.18) | copy-start | bytes 98308
  0.6 15.9 %copy-start.4 = (bf16[16,1024]{1,0:T(8,128)(2,1)S(1)}, bf16[16,1024]{1,0:T(8,128)(2,1)}, u32[]{:S(2)}) copy-start(bf16[16,1024]{1,0:T(8,128)(2,1)} %up_out.1) | copy-start | bytes 98308
  0.7 15.9 %copy-start.2 = (bf16[8192,16]{0,1:T(8,128)(2,1)S(1)}, bf16[8192,16]{0,1:T(8,128)(2,1)}, u32[]{:S(2)}) copy-start(bf16[8192,16]{0,1:T(8,128)(2,1)} %param.16) | copy-start | bytes 786436
  0.7 15.9 %copy-start.3 = (bf16[16,1024]{1,0:T(8,128)(2,1)S(1)}, bf16[16,1024]{1,0:T(8,128)(2,1)}, u32[]{:S(2)}) copy-start(bf16[16,1024]{1,0:T(8,128)(2,1)} %gate_out.1) | copy-start | bytes 98308
  0.7 15.9 %copy-start.1 = (bf16[8192,16]{0,1:T(8,128)(2,1)S(1)}, bf16[8192,16]{0,1:T(8,128)(2,1)}, u32[]{:S(2)}) copy-start(bf16[8192,16]{0,1:T(8,128)(2,1)} %param.14) | copy-start | bytes 786436
  0.7 15.9 %copy-start = (bf16[8192,1024]{1,0:T(8,128)(2,1)S(1)}, bf16[8192,1024]{1,0:T(8,128)(2,1)}, u32[]{:S(2)}) copy-start(bf16[8192,1024]{1,0:T(8,128)(2,1)} %up.1) | copy-start | bytes 50331652
  0.7 15.9 %slice-start = ((s8[16777216]{0:T(1024)(128)(4,1)}), s8[4194304]{0:T(1024)(128)(4,1)S(1)}, s32[]{:S(2)}) async-start(s8[16777216]{0:T(1024)(128)(4,1)} %bitcast.4), calls=%async_computation | async-start | bytes 8388608
  0.7 6.6 %collective-permute-start = (bf16[2,8192]{1,0:T(2,128)(2,1)}, bf16[2,8192]{1,0:T(2,128)(2,1)S(1)}, u32[]{:S(2)}, u32[]{:S(2)}) collective-permute-start(bf16[2,8192]{1,0:T(2,128)(2,1)} %source.1), channel_id=1, source_target_pairs={{0,8},{1,9},{2,10},{3,11},{4,12},{5,13},{6,14},{7,15},{8,0},{9,1},... | collective-permute-start | bytes 98312 | tf_op jit(solution)/shard_map/ppermute | solution.py:42
  6.4 10.2 %slice-start.1 = ((s8[16777216]{0:T(1024)(128)(4,1)}), s8[4194304]{0:T(1024)(128)(4,1)S(1)}, s32[]{:S(2)}) async-start(s8[16777216]{0:T(1024)(128)(4,1)} %bitcast.4), calls=%async_computation.1 | async-start | bytes 8388608
  7.3 9.3 %slice-start.2 = ((s8[16777216]{0:T(1024)(128)(4,1)}), s8[4194304]{0:T(1024)(128)(4,1)S(1)}, s32[]{:S(2)}) async-start(s8[16777216]{0:T(1024)(128)(4,1)} %bitcast.4), calls=%async_computation.2 | async-start | bytes 8388608
  7.3 9.3 %slice-start.3 = ((s8[16777216]{0:T(1024)(128)(4,1)}), s8[4194304]{0:T(1024)(128)(4,1)S(1)}, s32[]{:S(2)}) async-start(s8[16777216]{0:T(1024)(128)(4,1)} %bitcast.4), calls=%async_computation.3 | async-start | bytes 8388608
  7.3 5.2 %collective-permute-start.3 = (bf16[4,8192]{1,0:T(4,128)(2,1)S(1)}, bf16[4,8192]{1,0:T(4,128)(2,1)S(1)}, u32[]{:S(2)}, u32[]{:S(2)}) collective-permute-start(bf16[4,8192]{1,0:T(4,128)(2,1)S(1)} %merge.3.refs_0_), channel_id=1, source_target_pairs={{0,6},{1,7},{2,4},{3,5},{4,2},{5,3},{6,0},{7,1},{8,14},{9,15},{10,... | collective-permute-start | bytes 196616 | tf_op jit(solution)/shard_map/ppermute | solution.py:42
  9.9 4.3 %collective-permute-start.2 = (bf16[4,8192]{1,0:T(4,128)(2,1)S(1)}, bf16[4,8192]{1,0:T(4,128)(2,1)S(1)}, u32[]{:S(2)}, u32[]{:S(2)}) collective-permute-start(bf16[4,8192]{1,0:T(4,128)(2,1)S(1)} %merge.3.refs_0_), channel_id=1, source_target_pairs={{0,4},{1,5},{2,6},{3,7},{4,0},{5,1},{6,2},{7,3},{8,12},{9,13},{10,... | collective-permute-start | bytes 196616 | tf_op jit(solution)/shard_map/ppermute | solution.py:42
  10.5 4.3 %collective-permute-start.1 = (bf16[4,8192]{1,0:T(4,128)(2,1)S(1)}, bf16[4,8192]{1,0:T(4,128)(2,1)S(1)}, u32[]{:S(2)}, u32[]{:S(2)}) collective-permute-start(bf16[4,8192]{1,0:T(4,128)(2,1)S(1)} %merge.3.refs_0_), channel_id=1, source_target_pairs={{0,2},{1,3},{2,0},{3,1},{4,6},{5,7},{6,4},{7,5},{8,10},{9,11},{10,... | collective-permute-start | bytes 196616 | tf_op jit(solution)/shard_map/ppermute | solution.py:42
  14.9 1.6 %collective-permute-start.4 = (bf16[16,8192]{1,0:T(8,128)(2,1)S(1)}, bf16[16,8192]{1,0:T(8,128)(2,1)S(1)}, u32[]{:S(2)}, u32[]{:S(2)}) collective-permute-start(bf16[16,8192]{1,0:T(8,128)(2,1)S(1)} %merge.4.refs_0_), channel_id=1, source_target_pairs={{0,1},{1,0},{2,3},{3,2},{4,5},{5,4},{6,7},{7,6},{8,9},{9,8},{10,11... | collective-permute-start | bytes 786440 | tf_op jit(solution)/shard_map/ppermute | solution.py:42
  16.6 23.3 %copy-start.6 = (bf16[16,8192]{1,0:T(8,128)(2,1)S(1)}, bf16[16,8192]{1,0:T(8,128)(2,1)}, u32[]{:S(2)}) copy-start(bf16[16,8192]{1,0:T(8,128)(2,1)} %down_out.1) | copy-start | bytes 786436
  26.1 1.6 %collective-permute-start.5 = (bf16[16,8448]{1,0:T(8,128)(2,1)S(1)}, bf16[16,8448]{1,0:T(8,128)(2,1)S(1)}, u32[]{:S(2)}, u32[]{:S(2)}) collective-permute-start(bf16[16,8448]{1,0:T(8,128)(2,1)S(1)} %get-tuple-element.13), channel_id=1, source_target_pairs={{0,1},{1,0},{2,3},{3,2},{4,5},{5,4},{6,7},{7,6},{8,9},{9,8},{10,11... | collective-permute-start | bytes 811016 | tf_op jit(solution)/shard_map/ppermute | solution.py:42
  27.8 4.4 %collective-permute-start.6 = (bf16[4,8448]{1,0:T(4,128)(2,1)S(1)}, bf16[4,8448]{1,0:T(4,128)(2,1)S(1)}, u32[]{:S(2)}, u32[]{:S(2)}) collective-permute-start(bf16[4,8448]{1,0:T(4,128)(2,1)S(1)} %get-tuple-element.15), channel_id=1, source_target_pairs={{0,2},{1,3},{2,0},{3,1},{4,6},{5,7},{6,4},{7,5},{8,10},{9,11},{10,... | collective-permute-start | bytes 202760 | tf_op jit(solution)/shard_map/ppermute | solution.py:42
  28.2 4.3 %collective-permute-start.7 = (bf16[4,8448]{1,0:T(4,128)(2,1)S(1)}, bf16[4,8448]{1,0:T(4,128)(2,1)S(1)}, u32[]{:S(2)}, u32[]{:S(2)}) collective-permute-start(bf16[4,8448]{1,0:T(4,128)(2,1)S(1)} %get-tuple-element.16), channel_id=1, source_target_pairs={{0,4},{1,5},{2,6},{3,7},{4,0},{5,1},{6,2},{7,3},{8,12},{9,13},{10,... | collective-permute-start | bytes 202760 | tf_op jit(solution)/shard_map/ppermute | solution.py:42
  29.7 5.2 %collective-permute-start.8 = (bf16[4,8448]{1,0:T(4,128)(2,1)S(1)}, bf16[4,8448]{1,0:T(4,128)(2,1)S(1)}, u32[]{:S(2)}, u32[]{:S(2)}) collective-permute-start(bf16[4,8448]{1,0:T(4,128)(2,1)S(1)} %get-tuple-element.17), channel_id=1, source_target_pairs={{0,6},{1,7},{2,4},{3,5},{4,2},{5,3},{6,0},{7,1},{8,14},{9,15},{10,... | collective-permute-start | bytes 202760 | tf_op jit(solution)/shard_map/ppermute | solution.py:42
  35.0 4.9 %collective-permute-start.9 = (bf16[2,8448]{1,0:T(2,128)(2,1)S(1)}, bf16[2,8448]{1,0:T(2,128)(2,1)S(1)}, u32[]{:S(2)}, u32[]{:S(2)}) collective-permute-start(bf16[2,8448]{1,0:T(2,128)(2,1)S(1)} %get-tuple-element.19), channel_id=1, source_target_pairs={{0,8},{1,9},{2,10},{3,11},{4,12},{5,13},{6,14},{7,15},{8,0},{9,1},... | collective-permute-start | bytes 101384 | tf_op jit(solution)/shard_map/ppermute | solution.py:42

commit v4 on v3

--- a/solution.py
+++ b/solution.py
@@ -10,7 +10,7 @@
 MIB = 1 << 20
 LANES = 128
 FLOPS_PER_US = 10**9
-HOLD_US, MERGE_US = 2, (2, 4, 2)
+HOLD_US, MERGE_US = 3, (2, 5)
 F32, BF16 = jnp.float32, jnp.bfloat16
 WHOLE = pl.BlockSpec(memory_space=pltpu.VMEM)
 FAR = pl.BlockSpec(memory_space=pltpu.HBM)
@@ -35,7 +35,7 @@
 def rounds_of(size, along_x):
     masks = [1 << b for b in range(size.bit_length() - 1)]
     x, z = 2, 2 * along_x
-    return [[m] for m in reversed(masks) if m not in (1, x, z)] + [[x, z, x ^ z], [1]]
+    return [[m] for m in reversed(masks) if m not in (1, x, z)] + [[x ^ z, z, x], [1]]
 
 
 def swap(value, size, mask):
@@ -91,13 +91,13 @@
 
 
 def layer_kernel(
-    rows, gate, up, down, gate_in, gate_out, up_in, up_out, down_in, keep, send,
+    mine_a, mine_b, theirs_a, theirs_b, gate, up, down, gate_in, gate_out, up_in, up_out, down_in, keep, send,
     maps, gate_low, up_low, hidden, held, arrived,
 ):
     width, out_width = gate.shape[1], down.shape[1]
     copy = pltpu.make_async_copy(down, held, arrived)
     copy.start()
-    x = rows[...]
+    x = jnp.concatenate([mine_a[...], mine_b[...], theirs_a[...], theirs_b[...]], axis=0)
     across = (((1,), (1,)), ((), ()))
     rank = gate_in.shape[0]
     maps[:rank] = gate_in[...]
@@ -153,14 +153,16 @@
     width, out_width = gate.shape[1], down.shape[1]
     held = call(hold_kernel, jax.ShapeDtypeStruct(tokens.shape, tokens.dtype), [FAR], HOLD_US, "hold")(hbm(tokens))
     rows = tokens
-    for k, masks in enumerate(rounds):
-        theirs = [swap(rows, size, mask) for mask in masks]
-        rows = merge([held if k == 0 else rows] + theirs, MERGE_US[min(k, len(MERGE_US) - 1)])
-    count = rows.shape[0]
+    for k, masks in enumerate(rounds[:-2]):
+        rows = merge([held if k == 0 else rows, swap(rows, size, masks[0])], MERGE_US[0])
+    far, near, last = [swap(rows, size, mask) for mask in rounds[-2]]
+    mine = [merge([rows, far], 1), merge([near, last], MERGE_US[1])]
+    theirs = [swap(part, size, 1) for part in mine]
+    count = 8 * rows.shape[0]
     parts = call(
         layer_kernel,
         [jax.ShapeDtypeStruct((count // 2, out_width + 2 * LANES), BF16)] * 2,
-        [WHOLE] * 3 + [FAR] + [WHOLE] * 5,
+        [WHOLE] * 6 + [FAR] + [WHOLE] * 5,
         9,
         "layer",
         limit=down.size * 2 + (2 + count // 64 * 2) * MIB,
@@ -172,7 +174,7 @@
             pltpu.VMEM(down.shape, BF16),
             pltpu.SemaphoreType.DMA(()),
         ],
-    )(rows, vmem(gate), vmem(up), hbm(down), gate_in.T, gate_out, up_in.T, up_out, down_in.T)
+    )(*mine, *theirs, vmem(gate), vmem(up), hbm(down), gate_in.T, gate_out, up_in.T, up_out, down_in.T)
     for masks, after in zip(rounds[::-1], rounds[-2::-1]):
         theirs = [swap(part, size, mask) for part, mask in zip(parts[1:], masks)]
         parts = add([parts[0]] + theirs, 1 + len(after))

time: 40.9 us -> 40.6 us (level)
  Pallas kernels: 12.1 us -> 11.5 us
    pallas_call x1, Pallas kernels: 1.55 us -> 0.91 us  [body(): call(hold_kernel, jax.ShapeDtypeStruct(tokens.shape, tokens.dtype), [FAR]...]
    ppermute x10 -> x11, waiting for transfers between devices: 13.5 us -> 13.7 us  [swap(): return lax.ppermute(value, 'blk', [(i, i ^ mask) for i in range(size)])]
    ppermute x10 -> x11, starting transfers between devices: 14.3 us -> 14.5 us  [swap(): return lax.ppermute(value, 'blk', [(i, i ^ mask) for i in range(size)])]
  transfers between devices with their start and end apart: 10 -> 11, of which waited for: 10 -> 10; matrix products, arithmetic and copies ran while one was open for 0% -> 0% of each run, Pallas kernels for 4% -> 2%
where the time goes in v4:
time: 40.6 us; the launch traced here: 40.5 us
  starting transfers between devices  14.5 us (36%)
  waiting for transfers between devices  13.7 us (34%)
  Pallas kernels  11.5 us (28%)
  between operations  0.8 us (2%)
    ppermute x11, starting transfers between devices, swap(): return lax.ppermute(value, 'blk', [(i, i ^ mask) for i in range(size)])  14.5 us
    ppermute x11, waiting for transfers between devices, swap(): return lax.ppermute(value, 'blk', [(i, i ^ mask) for i in range(size)])  13.7 us
    pallas_call x1, Pallas kernels, body(): call(layer_kernel, [jax.ShapeDtypeStruct((count // 2, out_width + 2 * LAN...  9.52 us
    pallas_call x1, Pallas kernels, body(): call(hold_kernel, jax.ShapeDtypeStruct(tokens.shape, tokens.dtype), [FAR]...  0.91 us
    pallas_call x1, Pallas kernels, body(): call(last_kernel, [jax.ShapeDtypeStruct(tokens.shape, BF16), jax.ShapeDty...  0.88 us
  transfers between devices with their start and end apart: 11, of which 10 were waited for; matrix products, arithmetic and copies ran while one was open for 0% of the time, Pallas kernels for 2%

profile of v4, /device:TPU:0, one launch (start us, length us, event | category | flops | bytes accessed | tf_op | source)
XLA Modules:
  0.0 40.5 jit_solution(12391979370730779614)
XLA Ops:
  0.6 4.1 %collective-permute-start = (bf16[2,8192]{1,0:T(2,128)(2,1)}, bf16[2,8192]{1,0:T(2,128)(2,1)S(1)}, u32[]{:S(2)}, u32[]{:S(2)}) collective-permute-start(bf16[2,8192]{1,0:T(2,128)(2,1)} %source.1), channel_id=1, source_target_pairs={{0,8},{1,9},{2,10},{3,11},{4,12},{5,13},{6,14},{7,15},{8,0},{9,1},... | collective-permute-start | bytes 98312 | tf_op jit(solution)/shard_map/ppermute | solution.py:42
  4.7 0.9 %hold.1.refs_0_ = bf16[2,8192]{1,0:T(2,128)(2,1)S(1)} custom-call(bf16[2,8192]{1,0:T(2,128)(2,1)} %source.1), custom_call_target="tpu_custom_call" | custom-call | flops 3000000000 | tf_op jit(solution)/shard_map/hold/pallas_call | solution.py:154
  5.7 1.5 %collective-permute-done.refs_1_ = bf16[2,8192]{1,0:T(2,128)(2,1)S(1)} collective-permute-done((bf16[2,8192]{1,0:T(2,128)(2,1)}, bf16[2,8192]{1,0:T(2,128)(2,1)S(1)}, u32[]{:S(2)}, u32[]{:S(2)}) %collective-permute-start) | collective-permute-done | bytes 32800 | tf_op jit(solution)/shard_map/ppermute | solution.py:42
  7.2 2.5 %collective-permute-start.1 = (bf16[4,8192]{1,0:T(4,128)(2,1)S(1)}, bf16[4,8192]{1,0:T(4,128)(2,1)S(1)}, u32[]{:S(2)}, u32[]{:S(2)}) collective-permute-start(bf16[4,8192]{1,0:T(4,128)(2,1)S(1)} %merge.3.refs_0_), channel_id=1, source_target_pairs={{0,6},{1,7},{2,4},{3,5},{4,2},{5,3},{6,0},{7,1},{8,14},{9,15},{10,... | collective-permute-start | bytes 196616 | tf_op jit(solution)/shard_map/ppermute | solution.py:42
  9.8 0.5 %collective-permute-start.3 = (bf16[4,8192]{1,0:T(4,128)(2,1)S(1)}, bf16[4,8192]{1,0:T(4,128)(2,1)S(1)}, u32[]{:S(2)}, u32[]{:S(2)}) collective-permute-start(bf16[4,8192]{1,0:T(4,128)(2,1)S(1)} %merge.3.refs_0_), channel_id=1, source_target_pairs={{0,2},{1,3},{2,0},{3,1},{4,6},{5,7},{6,4},{7,5},{8,10},{9,11},{10,... | collective-permute-start | bytes 196616 | tf_op jit(solution)/shard_map/ppermute | solution.py:42
  10.3 0.5 %collective-permute-start.2 = (bf16[4,8192]{1,0:T(4,128)(2,1)S(1)}, bf16[4,8192]{1,0:T(4,128)(2,1)S(1)}, u32[]{:S(2)}, u32[]{:S(2)}) collective-permute-start(bf16[4,8192]{1,0:T(4,128)(2,1)S(1)} %merge.3.refs_0_), channel_id=1, source_target_pairs={{0,4},{1,5},{2,6},{3,7},{4,0},{5,1},{6,2},{7,3},{8,12},{9,13},{10,... | collective-permute-start | bytes 196616 | tf_op jit(solution)/shard_map/ppermute | solution.py:42
  10.8 2.2 %collective-permute-done.1.refs_1_ = bf16[4,8192]{1,0:T(4,128)(2,1)S(1)} collective-permute-done((bf16[4,8192]{1,0:T(4,128)(2,1)S(1)}, bf16[4,8192]{1,0:T(4,128)(2,1)S(1)}, u32[]{:S(2)}, u32[]{:S(2)}) %collective-permute-start.1) | collective-permute-done | bytes 65568 | tf_op jit(solution)/shard_map/ppermute | solution.py:42
  13.0 0.1 collective-permute-start.4
  13.1 1.0 %collective-permute-done.3.refs_1_ = bf16[4,8192]{1,0:T(4,128)(2,1)S(1)} collective-permute-done((bf16[4,8192]{1,0:T(4,128)(2,1)S(1)}, bf16[4,8192]{1,0:T(4,128)(2,1)S(1)}, u32[]{:S(2)}, u32[]{:S(2)}) %collective-permute-start.3) | collective-permute-done | bytes 65568 | tf_op jit(solution)/shard_map/ppermute | solution.py:42
  14.0 0.5 %collective-permute-done.2.refs_0_ = bf16[4,8192]{1,0:T(4,128)(2,1)S(1)} collective-permute-done((bf16[4,8192]{1,0:T(4,128)(2,1)S(1)}, bf16[4,8192]{1,0:T(4,128)(2,1)S(1)}, u32[]{:S(2)}, u32[]{:S(2)}) %collective-permute-start.2) | collective-permute-done | bytes 65568 | tf_op jit(solution)/shard_map/ppermute | solution.py:42
  14.7 1.3 %collective-permute-done.5.theirs_b = bf16[8,8192]{1,0:T(8,128)(2,1)S(1)} collective-permute-done((bf16[8,8192]{1,0:T(8,128)(2,1)S(1)}, bf16[8,8192]{1,0:T(8,128)(2,1)S(1)}, u32[]{:S(2)}, u32[]{:S(2)}) %collective-permute-start.5) | collective-permute-done | bytes 131104 | tf_op jit(solution)/shard_map/ppermute | solution.py:42
  16.1 9.5 %layer.1 = (bf16[16,8448]{1,0:T(8,128)(2,1)S(1)}, bf16[16,8448]{1,0:T(8,128)(2,1)S(1)}) custom-call(bf16[8,8192]{1,0:T(8,128)(2,1)S(1)} %merge.4.mine_a, bf16[8,8192]{1,0:T(8,128)(2,1)S(1)} %merge.5.mine_b, bf16[8,8192]{1,0:T(8,128)(2,1)S(1)} %collective-permute-done.4.theirs_a, bf16[8,8192]{1,0:T(8,128)(2,1)S(1)} %collective-permute-done.5.theirs_b, ...), custom_call_target="tpu_custom_call" | custom-call | flops 8999999488 | tf_op jit(solution)/shard_map/layer/pallas_call | solution.py:162
  25.7 0.2 collective-permute-start.6
  25.9 1.4 %collective-permute-done.6.refs_1_ = bf16[16,8448]{1,0:T(8,128)(2,1)S(1)} collective-permute-done((bf16[16,8448]{1,0:T(8,128)(2,1)S(1)}, bf16[16,8448]{1,0:T(8,128)(2,1)S(1)}, u32[]{:S(2)}, u32[]{:S(2)}) %collective-permute-start.6) | collective-permute-done | bytes 270368 | tf_op jit(solution)/shard_map/ppermute | solution.py:42
  27.3 0.1 add.2
  27.4 2.2 %collective-permute-start.7 = (bf16[4,8448]{1,0:T(4,128)(2,1)S(1)}, bf16[4,8448]{1,0:T(4,128)(2,1)S(1)}, u32[]{:S(2)}, u32[]{:S(2)}) collective-permute-start(bf16[4,8448]{1,0:T(4,128)(2,1)S(1)} %get-tuple-element.15), channel_id=1, source_target_pairs={{0,6},{1,7},{2,4},{3,5},{4,2},{5,3},{6,0},{7,1},{8,14},{9,15},{10,... | collective-permute-start | bytes 202760 | tf_op jit(solution)/shard_map/ppermute | solution.py:42
  29.6 0.8 %collective-permute-start.8 = (bf16[4,8448]{1,0:T(4,128)(2,1)S(1)}, bf16[4,8448]{1,0:T(4,128)(2,1)S(1)}, u32[]{:S(2)}, u32[]{:S(2)}) collective-permute-start(bf16[4,8448]{1,0:T(4,128)(2,1)S(1)} %get-tuple-element.16), channel_id=1, source_target_pairs={{0,4},{1,5},{2,6},{3,7},{4,0},{5,1},{6,2},{7,3},{8,12},{9,13},{10,... | collective-permute-start | bytes 202760 | tf_op jit(solution)/shard_map/ppermute | solution.py:42
  30.4 0.5 %collective-permute-start.9 = (bf16[4,8448]{1,0:T(4,128)(2,1)S(1)}, bf16[4,8448]{1,0:T(4,128)(2,1)S(1)}, u32[]{:S(2)}, u32[]{:S(2)}) collective-permute-start(bf16[4,8448]{1,0:T(4,128)(2,1)S(1)} %get-tuple-element.17), channel_id=1, source_target_pairs={{0,2},{1,3},{2,0},{3,1},{4,6},{5,7},{6,4},{7,5},{8,10},{9,11},{10,... | collective-permute-start | bytes 202760 | tf_op jit(solution)/shard_map/ppermute | solution.py:42
  30.9 2.3 %collective-permute-done.7.refs_1_ = bf16[4,8448]{1,0:T(4,128)(2,1)S(1)} collective-permute-done((bf16[4,8448]{1,0:T(4,128)(2,1)S(1)}, bf16[4,8448]{1,0:T(4,128)(2,1)S(1)}, u32[]{:S(2)}, u32[]{:S(2)}) %collective-permute-start.7) | collective-permute-done | bytes 67616 | tf_op jit(solution)/shard_map/ppermute | solution.py:42
  33.2 0.9 %collective-permute-done.8.refs_2_ = bf16[4,8448]{1,0:T(4,128)(2,1)S(1)} collective-permute-done((bf16[4,8448]{1,0:T(4,128)(2,1)S(1)}, bf16[4,8448]{1,0:T(4,128)(2,1)S(1)}, u32[]{:S(2)}, u32[]{:S(2)}) %collective-permute-start.8) | collective-permute-done | bytes 67616 | tf_op jit(solution)/shard_map/ppermute | solution.py:42
  34.1 0.6 %collective-permute-done.9.refs_3_ = bf16[4,8448]{1,0:T(4,128)(2,1)S(1)} collective-permute-done((bf16[4,8448]{1,0:T(4,128)(2,1)S(1)}, bf16[4,8448]{1,0:T(4,128)(2,1)S(1)}, u32[]{:S(2)}, u32[]{:S(2)}) %collective-permute-start.9) | collective-permute-done | bytes 67616 | tf_op jit(solution)/shard_map/ppermute | solution.py:42
  34.7 2.9 %collective-permute-start.10 = (bf16[2,8448]{1,0:T(2,128)(2,1)S(1)}, bf16[2,8448]{1,0:T(2,128)(2,1)S(1)}, u32[]{:S(2)}, u32[]{:S(2)}) collective-permute-start(bf16[2,8448]{1,0:T(2,128)(2,1)S(1)} %get-tuple-element.19), channel_id=1, source_target_pairs={{0,8},{1,9},{2,10},{3,11},{4,12},{5,13},{6,14},{7,15},{8,0},{9,1},... | collective-permute-start | bytes 101384 | tf_op jit(solution)/shard_map/ppermute | solution.py:42
  37.6 2.0 %collective-permute-done.10.theirs = bf16[2,8448]{1,0:T(2,128)(2,1)S(1)} collective-permute-done((bf16[2,8448]{1,0:T(2,128)(2,1)S(1)}, bf16[2,8448]{1,0:T(2,128)(2,1)S(1)}, u32[]{:S(2)}, u32[]{:S(2)}) %collective-permute-start.10) | collective-permute-done | bytes 33824 | tf_op jit(solution)/shard_map/ppermute | solution.py:42
  39.6 0.9 %last.1 = (bf16[2,8192]{1,0:T(2,128)(2,1)}, f32[1,2]{1,0:T(1,128)}) custom-call(bf16[2,8448]{1,0:T(2,128)(2,1)S(1)} %get-tuple-element.18.mine, bf16[2,8448]{1,0:T(2,128)(2,1)S(1)} %collective-permute-done.10.theirs, bf16[16,8192]{1,0:T(8,128)(2,1)S(1)} %copy-done.6), custom_call_target="tpu_custom_call" | custom-call | flops 1000000000 | tf_op jit(solution)/shard_map/last/pallas_call | solution.py:182
  (29 shorter events, 0.3 us)
Async XLA Ops:
  0.6 6.6 %collective-permute-start = (bf16[2,8192]{1,0:T(2,128)(2,1)}, bf16[2,8192]{1,0:T(2,128)(2,1)S(1)}, u32[]{:S(2)}, u32[]{:S(2)}) collective-permute-start(bf16[2,8192]{1,0:T(2,128)(2,1)} %source.1), channel_id=1, source_target_pairs={{0,8},{1,9},{2,10},{3,11},{4,12},{5,13},{6,14},{7,15},{8,0},{9,1},... | collective-permute-start | bytes 98312 | tf_op jit(solution)/shard_map/ppermute | solution.py:42
  4.7 11.3 %slice-start = ((s8[16777216]{0:T(1024)(128)(4,1)}), s8[4194304]{0:T(1024)(128)(4,1)S(1)}, s32[]{:S(2)}) async-start(s8[16777216]{0:T(1024)(128)(4,1)} %bitcast.4), calls=%async_computation | async-start | bytes 8388608
  4.7 11.3 %slice-start.1 = ((s8[16777216]{0:T(1024)(128)(4,1)}), s8[4194304]{0:T(1024)(128)(4,1)S(1)}, s32[]{:S(2)}) async-start(s8[16777216]{0:T(1024)(128)(4,1)} %bitcast.4), calls=%async_computation.1 | async-start | bytes 8388608
  5.6 10.4 %copy-start = (bf16[8192,1024]{1,0:T(8,128)(2,1)S(1)}, bf16[8192,1024]{1,0:T(8,128)(2,1)}, u32[]{:S(2)}) copy-start(bf16[8192,1024]{1,0:T(8,128)(2,1)} %up.1) | copy-start | bytes 50331652
  5.6 10.4 %copy-start.1 = (bf16[8192,16]{0,1:T(8,128)(2,1)S(1)}, bf16[8192,16]{0,1:T(8,128)(2,1)}, u32[]{:S(2)}) copy-start(bf16[8192,16]{0,1:T(8,128)(2,1)} %param.14) | copy-start | bytes 786436
  5.6 10.4 %copy-start.2 = (bf16[8192,16]{0,1:T(8,128)(2,1)S(1)}, bf16[8192,16]{0,1:T(8,128)(2,1)}, u32[]{:S(2)}) copy-start(bf16[8192,16]{0,1:T(8,128)(2,1)} %param.16) | copy-start | bytes 786436
  5.6 10.4 %copy-start.3 = (bf16[16,1024]{1,0:T(8,128)(2,1)S(1)}, bf16[16,1024]{1,0:T(8,128)(2,1)}, u32[]{:S(2)}) copy-start(bf16[16,1024]{1,0:T(8,128)(2,1)} %gate_out.1) | copy-start | bytes 98308
  5.7 10.4 %copy-start.4 = (bf16[16,1024]{1,0:T(8,128)(2,1)S(1)}, bf16[16,1024]{1,0:T(8,128)(2,1)}, u32[]{:S(2)}) copy-start(bf16[16,1024]{1,0:T(8,128)(2,1)} %up_out.1) | copy-start | bytes 98308
  5.7 10.4 %copy-start.5 = (bf16[1024,16]{0,1:T(8,128)(2,1)S(1)}, bf16[1024,16]{0,1:T(8,128)(2,1)}, u32[]{:S(2)}) copy-start(bf16[1024,16]{0,1:T(8,128)(2,1)} %param.18) | copy-start | bytes 98308
  7.2 8.9 %slice-start.2 = ((s8[16777216]{0:T(1024)(128)(4,1)}), s8[4194304]{0:T(1024)(128)(4,1)S(1)}, s32[]{:S(2)}) async-start(s8[16777216]{0:T(1024)(128)(4,1)} %bitcast.4), calls=%async_computation.2 | async-start | bytes 8388608
  7.2 5.7 %collective-permute-start.1 = (bf16[4,8192]{1,0:T(4,128)(2,1)S(1)}, bf16[4,8192]{1,0:T(4,128)(2,1)S(1)}, u32[]{:S(2)}, u32[]{:S(2)}) collective-permute-start(bf16[4,8192]{1,0:T(4,128)(2,1)S(1)} %merge.3.refs_0_), channel_id=1, source_target_pairs={{0,6},{1,7},{2,4},{3,5},{4,2},{5,3},{6,0},{7,1},{8,14},{9,15},{10,... | collective-permute-start | bytes 196616 | tf_op jit(solution)/shard_map/ppermute | solution.py:42
  9.8 4.3 %collective-permute-start.3 = (bf16[4,8192]{1,0:T(4,128)(2,1)S(1)}, bf16[4,8192]{1,0:T(4,128)(2,1)S(1)}, u32[]{:S(2)}, u32[]{:S(2)}) collective-permute-start(bf16[4,8192]{1,0:T(4,128)(2,1)S(1)} %merge.3.refs_0_), channel_id=1, source_target_pairs={{0,2},{1,3},{2,0},{3,1},{4,6},{5,7},{6,4},{7,5},{8,10},{9,11},{10,... | collective-permute-start | bytes 196616 | tf_op jit(solution)/shard_map/ppermute | solution.py:42
  10.3 4.3 %collective-permute-start.2 = (bf16[4,8192]{1,0:T(4,128)(2,1)S(1)}, bf16[4,8192]{1,0:T(4,128)(2,1)S(1)}, u32[]{:S(2)}, u32[]{:S(2)}) collective-permute-start(bf16[4,8192]{1,0:T(4,128)(2,1)S(1)} %merge.3.refs_0_), channel_id=1, source_target_pairs={{0,4},{1,5},{2,6},{3,7},{4,0},{5,1},{6,2},{7,3},{8,12},{9,13},{10,... | collective-permute-start | bytes 196616 | tf_op jit(solution)/shard_map/ppermute | solution.py:42
  13.0 3.1 %slice-start.3 = ((s8[16777216]{0:T(1024)(128)(4,1)}), s8[4194304]{0:T(1024)(128)(4,1)S(1)}, s32[]{:S(2)}) async-start(s8[16777216]{0:T(1024)(128)(4,1)} %bitcast.4), calls=%async_computation.3 | async-start | bytes 8388608
  13.0 1.7 %collective-permute-start.4 = (bf16[8,8192]{1,0:T(8,128)(2,1)S(1)}, bf16[8,8192]{1,0:T(8,128)(2,1)S(1)}, u32[]{:S(2)}, u32[]{:S(2)}) collective-permute-start(bf16[8,8192]{1,0:T(8,128)(2,1)S(1)} %merge.4.mine_a), channel_id=1, source_target_pairs={{0,1},{1,0},{2,3},{3,2},{4,5},{5,4},{6,7},{7,6},{8,9},{9,8},{10,11... | collective-permute-start | bytes 393224 | tf_op jit(solution)/shard_map/ppermute | solution.py:42
  14.6 1.4 %collective-permute-start.5 = (bf16[8,8192]{1,0:T(8,128)(2,1)S(1)}, bf16[8,8192]{1,0:T(8,128)(2,1)S(1)}, u32[]{:S(2)}, u32[]{:S(2)}) collective-permute-start(bf16[8,8192]{1,0:T(8,128)(2,1)S(1)} %merge.5.mine_b), channel_id=1, source_target_pairs={{0,1},{1,0},{2,3},{3,2},{4,5},{5,4},{6,7},{7,6},{8,9},{9,8},{10,11... | collective-permute-start | bytes 393224 | tf_op jit(solution)/shard_map/ppermute | solution.py:42
  16.1 23.5 %copy-start.6 = (bf16[16,8192]{1,0:T(8,128)(2,1)S(1)}, bf16[16,8192]{1,0:T(8,128)(2,1)}, u32[]{:S(2)}) copy-start(bf16[16,8192]{1,0:T(8,128)(2,1)} %down_out.1) | copy-start | bytes 786436
  25.7 1.6 %collective-permute-start.6 = (bf16[16,8448]{1,0:T(8,128)(2,1)S(1)}, bf16[16,8448]{1,0:T(8,128)(2,1)S(1)}, u32[]{:S(2)}, u32[]{:S(2)}) collective-permute-start(bf16[16,8448]{1,0:T(8,128)(2,1)S(1)} %get-tuple-element.13), channel_id=1, source_target_pairs={{0,1},{1,0},{2,3},{3,2},{4,5},{5,4},{6,7},{7,6},{8,9},{9,8},{10,11... | collective-permute-start | bytes 811016 | tf_op jit(solution)/shard_map/ppermute | solution.py:42
  27.4 5.8 %collective-permute-start.7 = (bf16[4,8448]{1,0:T(4,128)(2,1)S(1)}, bf16[4,8448]{1,0:T(4,128)(2,1)S(1)}, u32[]{:S(2)}, u32[]{:S(2)}) collective-permute-start(bf16[4,8448]{1,0:T(4,128)(2,1)S(1)} %get-tuple-element.15), channel_id=1, source_target_pairs={{0,6},{1,7},{2,4},{3,5},{4,2},{5,3},{6,0},{7,1},{8,14},{9,15},{10,... | collective-permute-start | bytes 202760 | tf_op jit(solution)/shard_map/ppermute | solution.py:42
  29.6 4.5 %collective-permute-start.8 = (bf16[4,8448]{1,0:T(4,128)(2,1)S(1)}, bf16[4,8448]{1,0:T(4,128)(2,1)S(1)}, u32[]{:S(2)}, u32[]{:S(2)}) collective-permute-start(bf16[4,8448]{1,0:T(4,128)(2,1)S(1)} %get-tuple-element.16), channel_id=1, source_target_pairs={{0,4},{1,5},{2,6},{3,7},{4,0},{5,1},{6,2},{7,3},{8,12},{9,13},{10,... | collective-permute-start | bytes 202760 | tf_op jit(solution)/shard_map/ppermute | solution.py:42
  30.4 4.3 %collective-permute-start.9 = (bf16[4,8448]{1,0:T(4,128)(2,1)S(1)}, bf16[4,8448]{1,0:T(4,128)(2,1)S(1)}, u32[]{:S(2)}, u32[]{:S(2)}) collective-permute-start(bf16[4,8448]{1,0:T(4,128)(2,1)S(1)} %get-tuple-element.17), channel_id=1, source_target_pairs={{0,2},{1,3},{2,0},{3,1},{4,6},{5,7},{6,4},{7,5},{8,10},{9,11},{10,... | collective-permute-start | bytes 202760 | tf_op jit(solution)/shard_map/ppermute | solution.py:42
  34.7 4.9 %collective-permute-start.10 = (bf16[2,8448]{1,0:T(2,128)(2,1)S(1)}, bf16[2,8448]{1,0:T(2,128)(2,1)S(1)}, u32[]{:S(2)}, u32[]{:S(2)}) collective-permute-start(bf16[2,8448]{1,0:T(2,128)(2,1)S(1)} %get-tuple-element.19), channel_id=1, source_target_pairs={{0,8},{1,9},{2,10},{3,11},{4,12},{5,13},{6,14},{7,15},{8,0},{9,1},... | collective-permute-start | bytes 101384 | tf_op jit(solution)/shard_map/ppermute | solution.py:42
